TPU v7x, 512 devices: a whole 4x4x16 slice. The times are simulated.
512 devices in a mesh: blk: 64 (over z_lo, y, core), rep: 8 (over x, z_hi).
Axes of the slice: x: 4, y: 4, z: 16 (z_hi: 2, z_lo: 8; z = z_hi * 8 + z_lo), core: 2. Of those that a mesh axis runs over, the one named last changes fastest.
Arguments:
- qm_pos: float32 [3, 8192], P(None, 'blk'), may hold values from -4 to 4
- species: int32 [8192], P('blk'), may hold values from 0 to 7
- qm_count: int32 [64], P('blk'), may hold values from 64 to 128, as said below
- ghost_owner: int32 [8192, 4], P('blk'), may hold values from 0 to 63, all different within a row; in each aligned block of 128 rows (0 to 127, 128 to 255, ...) at most 16 rows name the same one
- ghost_slot: int32 [8192, 4], P('blk'), may hold values from 0 to 127
- mm_pos: float32 [3, 262144], P(None, ('blk', 'rep')), may hold values from -4 to 4
- mm_charge: float32 [262144], P(('blk', 'rep')), may hold values from -6 to 6
- species_table: bfloat16 [8, 128], replicated, may hold values from -6 to 6
- potential_gain: float32 [128], replicated, may hold values from -8 to 8
- message_weight: bfloat16 [128, 128], replicated, may hold values from -0.25 to 0.25
- hidden_weight: bfloat16 [128, 256], replicated, may hold values from -0.5 to 0.5
- energy_readout: float32 [256], replicated, may hold values from -0.375 to 0.375
- charge_readout: float32 [256], replicated, may hold values from -0.375 to 0.375
Outputs:
- atom_energy: float32 [8192], P('blk')
- qm_force: float32 [3, 8192], P(None, 'blk')
- mm_force: float32 [3, 262144], P(None, ('blk', 'rep'))
Inputs may be any that keep to these rules, and one draw needn't show every extreme that they name: `qm_count`: some block holds exactly 128 live atoms. `ghost_owner`: each row names 4 different blocks; among the rows of one device no block is named more than 16 times, and some block exactly 16 times.
All inputs are finite; a program needn't handle non-finite values.
Results may differ from a plain program's by a relative error of at most 0.0055.
Values may be sent and summed in bfloat16 or wider, within the bound.
A program may use at most 64 MiB of HBM per device.

v0:
```python
import math

import jax
import jax.numpy as jnp
from jax import lax
from jax.sharding import PartitionSpec as P

SOFTEN = 0.25


def pair_parts(qm_places, mm_places):
    offset = qm_places[:, :, None] - mm_places[:, None, :]
    inverse = lax.rsqrt(jnp.sum(offset * offset, axis=0) + SOFTEN)
    return (offset, inverse)


def split_columns(stacked, limit):
    stride = math.gcd(stacked.shape[1], limit)
    shaped = stacked.reshape(stacked.shape[0], stacked.shape[1] // stride, stride)
    return jnp.transpose(shaped, (1, 0, 2))


def potential_from(qm_places, mm_stack):

    def potential_advance(running, columns):
        offset, inverse = pair_parts(qm_places, columns[:3])
        return (running + jnp.sum(inverse * columns[3][None, :], axis=1), None)

    result, _ = lax.scan(
        potential_advance,
        jnp.zeros((qm_places.shape[1],), jnp.float32),
        split_columns(mm_stack, 512),
    )
    return result


def on_device(
    qm_pos,
    species,
    qm_count,
    ghost_owner,
    ghost_slot,
    mm_pos,
    mm_charge,
    species_table,
    potential_gain,
    message_weight,
    hidden_weight,
    energy_readout,
    charge_readout,
):
    atom_rows = qm_pos.shape[1]
    blocks = lax.axis_size("blk")
    neighbours = ghost_owner.shape[1]
    channels = species_table.shape[1]
    capacity = 2 * atom_rows * neighbours // blocks
    coupling = float(mm_pos.shape[1] * blocks * lax.axis_size("rep")) ** (-0.5)
    mm_stack = jnp.concatenate([mm_pos, mm_charge[None, :]], axis=0)
    partial_sum = potential_from(qm_pos, lax.all_gather(mm_stack, "blk", axis=1, tiled=True))
    potential = lax.psum(partial_sum, "rep") * coupling
    live = (jnp.arange(atom_rows) < qm_count[0]).astype(jnp.float32)
    picks = (species[:, None] == jnp.arange(species_table.shape[0])[None, :]).astype(jnp.bfloat16)
    base = jnp.dot(picks, species_table, preferred_element_type=jnp.float32)
    start = (live[:, None] * (base + potential[:, None] * potential_gain[None, :])).astype(
        jnp.bfloat16
    )
    owners = ghost_owner.reshape(-1)
    slots = ghost_slot.reshape(-1)
    hits = (owners[:, None] == jnp.arange(blocks)[None, :]).astype(jnp.int32)
    ranks = jnp.sum((jnp.cumsum(hits, axis=0) - hits) * hits, axis=1)
    request = jnp.zeros((blocks, capacity), jnp.int32).at[owners, ranks].set(slots)
    wanted = lax.all_to_all(request, "blk", split_axis=0, concat_axis=0, tiled=True)
    outgoing = jnp.take(start, wanted, axis=0)
    arrived = lax.all_to_all(outgoing, "blk", split_axis=0, concat_axis=0, tiled=True)
    ghosts = arrived[owners, ranks]
    neighbour = jnp.sum(
        ghosts.reshape(atom_rows, neighbours, channels).astype(jnp.float32), axis=1
    ).astype(jnp.bfloat16)
    mixed = start.astype(jnp.float32) + jnp.dot(
        neighbour, message_weight, preferred_element_type=jnp.float32
    )
    before = jnp.dot(mixed.astype(jnp.bfloat16), hidden_weight, preferred_element_type=jnp.float32)
    sigma = jax.nn.sigmoid(before)
    active = before * sigma
    energy_part = live * jnp.sum(active * energy_readout[None, :], axis=1)
    charge_part = live * jnp.sum(active * charge_readout[None, :], axis=1)
    atom_energy = energy_part + charge_part * potential
    back_active = live[:, None] * (
        energy_readout[None, :] + potential[:, None] * charge_readout[None, :]
    )
    back_before = (back_active * sigma * (1.0 + before * (1.0 - sigma))).astype(jnp.bfloat16)
    back_mixed = jnp.dot(back_before, hidden_weight.T, preferred_element_type=jnp.float32)
    back_sum = jnp.dot(
        back_mixed.astype(jnp.bfloat16), message_weight.T, preferred_element_type=jnp.float32
    ).astype(jnp.bfloat16)
    outgoing_grads = (
        jnp.zeros((blocks, capacity, channels), jnp.bfloat16)
        .at[owners, ranks]
        .set(jnp.repeat(back_sum, neighbours, axis=0))
    )
    returned = lax.all_to_all(outgoing_grads, "blk", split_axis=0, concat_axis=0, tiled=True)
    picks_back = (wanted.reshape(-1)[:, None] == jnp.arange(atom_rows)[None, :]).astype(
        jnp.bfloat16
    )
    collected = jnp.einsum(
        "ra,rf->af",
        picks_back,
        returned.reshape(blocks * capacity, channels),
        preferred_element_type=jnp.float32,
    )
    back_start = back_mixed + collected
    effective = charge_part + live * jnp.sum(back_start * potential_gain[None, :], axis=1)
    qm_stack = jnp.concatenate([qm_pos, effective[None, :]], axis=0)
    portion = lax.all_gather(qm_stack, "blk", axis=1, tiled=True)
    mm_running = jnp.zeros((3, mm_pos.shape[1]), jnp.float32)

    def add_advance(running, group):
        offset, inverse = pair_parts(group[:3], mm_pos)
        weight = inverse * inverse * inverse * mm_charge[None, :]
        pull = jnp.sum(offset * weight[None], axis=2) * group[3][None, :]
        running = running - jnp.sum(offset * (weight * group[3][:, None])[None], axis=1)
        return (running, pull)

    mm_running, pulls = lax.scan(add_advance, mm_running, split_columns(portion, 512))
    block_terms = jnp.transpose(pulls, (1, 0, 2)).reshape(3, portion.shape[1])
    qm_terms = block_terms
    mm_sum, qm_terms = (mm_running, qm_terms)
    block_force = lax.psum_scatter(qm_terms, "blk", scatter_dimension=1, tiled=True)
    qm_force = lax.psum(block_force, "rep") * coupling
    return (atom_energy, qm_force, mm_sum * coupling)


def solution(mesh):
    placed = (
        P(None, "blk"),
        P("blk"),
        P("blk"),
        P("blk", None),
        P("blk", None),
        P(None, ("blk", "rep")),
        P(("blk", "rep")),
        P(),
        P(),
        P(),
        P(),
        P(),
        P(),
    )
    return jax.shard_map(
        on_device,
        mesh=mesh,
        in_specs=placed,
        out_specs=(P("blk"), P(None, "blk"), P(None, ("blk", "rep"))),
        check_vma=False,
    )
```

profile of v0, /device:TPU:1, one launch (start us, length us, event | category | flops | bytes accessed | tf_op | source)
XLA Modules:
  0.0 966.9 jit_solution(517936190505704173)
XLA Ops:
  7.2 0.8 copy.42
  8.4 0.8 copy.46
  9.3 1.2 reduce-window.6
  11.0 25.2 %scatter_fusion = s32[64,16]{0,1:T(8,128)S(1)} fusion(s32[64,16]{0,1:T(8,128)S(1)} %broadcast_in_dim.31, s32[512]{0:T(512)S(1)} %bitcast.84, s32[512]{0:T(512)S(1)} %reshape.281), kind=kCustom, calls=%fused_computation.2 | custom fusion | bytes 10240 | tf_op jit(solution)/shard_map/scatter | solution.py:71
  36.1 0.7 copy.47
  36.8 17.2 %all-to-all-start = ((s32[64,1,16]{2,1,0:T(1,128)}), s32[64,1,16]{2,1,0:T(1,128)S(1)}, u32[]{:S(2)}, u32[]{:S(2)}) async-start(s32[64,1,16]{2,1,0:T(1,128)} %copy.47), calls=%async_computation | async-start | bytes 65536 | tf_op jit(solution)/shard_map/all_to_all | solution.py:72
  54.8 124.4 %all_gather.6 = f32[4,32768]{1,0:T(4,128)S(1)} all-gather(f32[4,512]{1,0:T(4,128)S(1)} %pad_maximum_fusion), channel_id=1, replica_groups=mesh['blk'=64,'rep'=8] {'blk'}, dimensions={1}, use_global_device_ids=true | all-gather | bytes 532480 | tf_op jit(solution)/shard_map/all_gather | solution.py:59
  179.1 21.4 %while.24 = (s32[]{:T(128)}, f32[128]{0:T(128)S(1)}, f32[3,128]{1,0:T(4,128)S(1)}, f32[64,4,512]{2,1,0:T(4,128)S(1)}, s32[]{:T(128)}, /*index=5*/s32[]{:T(128)}, s32[]{}) while((s32[]{:T(128)}, f32[128]{0:T(128)S(1)}, f32[3,128]{1,0:T(4,128)S(1)}, f32[64,4,512]{2,1,0:T(4,128)S(1)}, s32[]{:T(128)}, /*index=5*/s32[]{:T(128)}, ...), condition=%wide.region_3.4_spmd.clone, body=%wide.region_0.3_spmd.clone.sunk | while | flops 721028 | bytes 552567 | solution.py:29
  200.6 38.2 %psum.14 = f32[128]{0:T(128)S(1)} all-reduce(f32[128]{0:T(128)S(1)} %get-tuple-element.58), channel_id=1, replica_groups=mesh['blk'=64,'rep'=8] {'rep'}, use_global_device_ids=true, to_apply=%region_4.5 | all-reduce | flops 128 | bytes 1024 | tf_op jit(solution)/shard_map/psum | solution.py:60
  239.3 3.2 gather_fusion
  242.8 27.1 %all_to_all.25 = bf16[64,16,128]{2,1,0:T(8,128)(2,1)S(1)} all-to-all(bf16[64,16,128]{2,1,0:T(8,128)(2,1)S(1)} %broadcast_select_fusion.1), channel_id=1, replica_groups=mesh['blk'=64,'rep'=8] {'blk'}, dimensions={0} | all-to-all | bytes 524288 | tf_op jit(solution)/shard_map/all_to_all | solution.py:74
  269.9 3.2 gather_fusion.1
  273.3 0.4 multiply_reduce_fusion.3
  274.2 0.7 broadcast_in_dim.37
  274.9 51.5 %scatter_fusion.1 = bf16[64,16,128]{2,1,0:T(8,128)(2,1)} fusion(bf16[64,16,128]{2,1,0:T(8,128)(2,1)} %broadcast_in_dim.37, s32[512]{0:T(512)S(1)} %bitcast.85, bf16[512,128]{1,0:T(8,128)(2,1)S(1)} %bitcast.90), kind=kCustom, calls=%fused_computation.3 | custom fusion | bytes 397312 | tf_op jit(solution)/shard_map/scatter | solution.py:99
  326.3 6.0 all-to-all-start.2
  332.4 0.5 broadcast.292
  332.9 0.7 reduce.6
  333.8 0.5 multiply_add_fusion
  334.3 17.8 %all-to-all-done.2 = bf16[64,16,128]{2,1,0:T(8,128)(2,1)S(1)} async-done(((bf16[64,16,128]{2,1,0:T(8,128)(2,1)}), bf16[64,16,128]{2,1,0:T(8,128)(2,1)S(1)}, u32[]{:S(2)}, u32[]{:S(2)}) %all-to-all-start.2) | async-done | bytes 262176 | tf_op jit(solution)/shard_map/all_to_all | solution.py:101
  352.2 0.6 fusion.10
  352.8 115.9 %all_gather.7 = f32[4,8192]{1,0:T(4,128)S(1)} all-gather(f32[4,128]{1,0:T(4,128)S(1)} %pad_maximum_fusion.1), channel_id=1, replica_groups=mesh['blk'=64,'rep'=8] {'blk'}, dimensions={1}, use_global_device_ids=true | all-gather | bytes 133120 | tf_op jit(solution)/shard_map/all_gather | solution.py:114
  468.7 25.5 %while.25 = (s32[]{:T(128)}, f32[3,512]{1,0:T(4,128)S(1)}, f32[16,3,512]{2,1,0:T(4,128)S(1)}, f32[16,4,512]{2,1,0:T(4,128)S(1)}, f32[3,512]{1,0:T(4,128)S(1)}, /...) while((s32[]{:T(128)}, f32[3,512]{1,0:T(4,128)S(1)}, f32[16,3,512]{2,1,0:T(4,128)S(1)}, ...), condition=%wide.region_18.19_spmd.clone, body=%wide.region_14.18_spmd.clone.sunk | while | flops 7341572 | bytes 6385803 | solution.py:124
  468.7 0.4 fusion.39
  469.3 0.9 fusion.40
  470.3 0.4 fusion.39
  470.9 0.9 fusion.40
  471.9 0.4 fusion.39
  472.4 0.9 fusion.40
  474.0 0.9 fusion.40
  475.6 0.9 fusion.40
  477.2 0.9 fusion.40
  478.8 0.9 fusion.40
  480.4 0.9 fusion.40
  482.0 0.9 fusion.40
  483.6 0.9 fusion.40
  485.2 0.9 fusion.40
  486.8 0.9 fusion.40
  488.4 0.9 fusion.40
  490.0 0.9 fusion.40
  491.6 0.9 fusion.40
  493.2 0.9 fusion.40
  494.1 2.6 copy.54
  496.8 0.6 broadcast_multiply_fusion.1
  497.4 420.3 %reduce-scatter.4.cloned.1.call-done = f32[128,3]{1,0:T(8,128)} async-done(((f32[8192,3]{1,0:T(8,128)}), f32[128,3]{1,0:T(8,128)}) %reduce-scatter.4.cloned.1.call-update) | async-done | bytes 1552
  917.7 0.9 copy.55
  918.6 40.8 %psum.15 = f32[3,128]{1,0:T(4,128)S(1)} all-reduce(f32[3,128]{1,0:T(4,128)S(1)} %copy.55), channel_id=1, replica_groups=mesh['blk'=64,'rep'=8] {'rep'}, use_global_device_ids=true, to_apply=%region_20.21 | all-reduce | flops 384 | bytes 3072 | tf_op jit(solution)/shard_map/psum | solution.py:129
  959.4 0.6 broadcast_multiply_fusion.2
  (469 shorter events, 30.6 us)
Async XLA Ops:
  7.2 266.1 %copy-start = (bf16[128,256]{1,0:T(8,128)(2,1)S(1)}, bf16[128,256]{1,0:T(8,128)(2,1)}, u32[]{:S(2)}) copy-start(bf16[128,256]{1,0:T(8,128)(2,1)} %param.27) | copy-start | bytes 196612
  7.2 47.6 %copy-start.1 = (f32[3,512]{1,0:T(4,128)S(1)}, f32[3,512]{1,0:T(4,128)}, u32[]{:S(2)}) copy-start(f32[3,512]{1,0:T(4,128)} %param.22) | copy-start | bytes 18436
  7.2 47.6 %copy-start.3 = (f32[512]{0:T(512)S(1)}, f32[512]{0:T(512)}, u32[]{:S(2)}) copy-start(f32[512]{0:T(512)} %param.23) | copy-start | bytes 6148
  7.2 171.9 %copy-start.2 = (f32[3,128]{1,0:T(4,128)S(1)}, f32[3,128]{1,0:T(4,128)}, u32[]{:S(2)}) copy-start(f32[3,128]{1,0:T(4,128)} %param.17) | copy-start | bytes 4612
  10.9 227.9 %copy-start.5 = (bf16[8,128]{1,0:T(8,128)(2,1)S(1)}, bf16[8,128]{1,0:T(8,128)(2,1)}, u32[]{:S(2)}) copy-start(bf16[8,128]{1,0:T(8,128)(2,1)} %param.24) | copy-start | bytes 6148
  10.9 227.9 %copy-start.8 = (s32[128]{0:T(128)S(1)}, s32[128]{0:T(128)}, u32[]{:S(2)}) copy-start(s32[128]{0:T(128)} %param.18) | copy-start | bytes 1540
  11.0 227.9 %copy-start.9 = (f32[128]{0:T(128)S(1)}, f32[128]{0:T(128)}, u32[]{:S(2)}) copy-start(f32[128]{0:T(128)} %param.25) | copy-start | bytes 1540
  36.8 202.2 %all-to-all-start = ((s32[64,1,16]{2,1,0:T(1,128)}), s32[64,1,16]{2,1,0:T(1,128)S(1)}, u32[]{:S(2)}, u32[]{:S(2)}) async-start(s32[64,1,16]{2,1,0:T(1,128)} %copy.47), calls=%async_computation | async-start | bytes 65536 | tf_op jit(solution)/shard_map/all_to_all | solution.py:72
  200.6 72.7 %copy-start.4 = (bf16[128,128]{1,0:T(8,128)(2,1)S(1)}, bf16[128,128]{1,0:T(8,128)(2,1)}, u32[]{:S(2)}) copy-start(bf16[128,128]{1,0:T(8,128)(2,1)} %param.26) | copy-start | bytes 98308
  200.6 72.7 %copy-start.6 = (f32[256]{0:T(256)S(1)}, f32[256]{0:T(256)}, u32[]{:S(2)}) copy-start(f32[256]{0:T(256)} %param.28) | copy-start | bytes 3076
  200.6 72.7 %copy-start.7 = (f32[256]{0:T(256)S(1)}, f32[256]{0:T(256)}, u32[]{:S(2)}) copy-start(f32[256]{0:T(256)} %param.29) | copy-start | bytes 3076
  326.3 25.8 %all-to-all-start.2 = ((bf16[64,16,128]{2,1,0:T(8,128)(2,1)}), bf16[64,16,128]{2,1,0:T(8,128)(2,1)S(1)}, u32[]{:S(2)}, u32[]{:S(2)}) async-start(bf16[64,16,128]{2,1,0:T(8,128)(2,1)} %scatter_fusion.1), calls=%async_computation.2 | async-start | bytes 524288 | tf_op jit(solution)/shard_map/all_to_all | solution.py:101
  332.3 585.4 %reduce-scatter.4.cloned.1.call-start = ((), (), s32[]{:S(2)}) async-start(), calls=%async_computation.4 | async-start | bytes 4259840
Sparse Core Ops, SparseCore 0:
  496.9 420.7 reduce-scatter.3
where the time goes:
time: 972 us; the launch traced here: 967 us
  waiting for transfers between devices  438 us (45%)
  blocking collectives  346 us (36%)
  local copies, waits for them, and re-layouts  93 us (10%)
  other arithmetic  46.4 us (5%)
  starting transfers between devices  23.2 us (2%)
  between operations  15 us (2%)
    unnamed x2, waiting for transfers between devices  420 us
    all_gather x1, blocking collectives, on_device(): lax.all_gather(mm_stack, 'blk', axis=1, tiled=True)  124 us
    all_gather x1, blocking collectives, on_device(): portion = lax.all_gather(qm_stack, 'blk', axis=1, tiled=True)  116 us
    scatter x1, local copies, waits for them, and re-layouts, on_device(): outgoing_grads = jnp.zeros((blocks, capacity, channels), jnp.bfloat16).at...  51.5 us
    psum x1, blocking collectives, on_device(): qm_force = lax.psum(block_force, 'rep') * coupling  40.8 us
    psum x1, blocking collectives, on_device(): potential = lax.psum(partial_sum, 'rep') * coupling  38.2 us
    all_to_all x1, blocking collectives, on_device(): lax.all_to_all(outgoing, 'blk', split_axis=0, concat_axis=0, tiled=True)  27.1 us
    scatter x1, local copies, waits for them, and re-layouts, on_device(): jnp.zeros((blocks, capacity), jnp.int32).at[owners, ranks].set(slots)  25.2 us
  transfers between devices with their start and end apart: 3, of which 2 were waited for; matrix products, arithmetic and copies ran while one was open for 2% of the time, Pallas kernels for 0%

commit v1 on v0

v1 whole, which is shorter than its diff:
```python
import functools

import jax
import jax.numpy as jnp
from jax import lax
from jax.experimental import pallas as pl
from jax.experimental.pallas import tpu as pltpu
from jax.sharding import PartitionSpec as P

SOFTEN = 0.25
LANES = 128
POT_ROWS = 64
FORCE_ROWS = 32
MESH = pl.DeviceIdType.MESH
F32 = jnp.float32
BF16 = jnp.bfloat16

MM_Z, QM_Q, POT_Q, POT_R, POT_Z, GRAD_Z, GRAD_Q, MMF_Z, QMF_Q, QMF_R = range(10)


def split3(value):
    high = value.astype(BF16)
    rest = value - high.astype(F32)
    middle = rest.astype(BF16)
    low = (rest - middle.astype(F32)).astype(BF16)
    return high, middle, low


def kernel(
    nz,
    nq,
    nr,
    coupling,
    qm_ref,
    species_ref,
    count_ref,
    owner_ref,
    slot_ref,
    mm_ref,
    charge_ref,
    table_ref,
    gain_ref,
    message_ref,
    hidden_ref,
    energy_ref,
    readout_ref,
    atom_energy_ref,
    qm_force_ref,
    mm_force_ref,
    mm_all,
    qm_all,
    pot_q,
    pot_r,
    pot_z,
    grad_mine,
    grad_z,
    grad_sum,
    grad_q,
    mmf_mine,
    mmf_z,
    qmf_mine,
    qmf_q,
    qmf_r,
    wide_x,
    wide_y,
    wide_z,
    wide_e,
    acc_x,
    acc_y,
    acc_z,
    table_wide,
    owner_hot,
    owner_hot_t,
    slot_hot,
    send_sems,
    recv_sems,
):
    blk = lax.axis_index("blk")
    rep = lax.axis_index("rep")
    z = blk // nq
    q = blk % nq
    atoms = qm_ref.shape[1]
    mm_tiles = mm_ref.shape[1] // LANES
    blocks = nz * nq
    neighbours = owner_ref.shape[1]

    along_z = (nz, z, lambda p: (p * nq + q, rep))
    along_q = (nq, q, lambda p: (z * nq + p, rep))
    along_r = (nr, rep, lambda p: (blk, p))

    def copy_to(stage, axis, d, src, dst):
        size, mine, device = axis
        return pltpu.make_async_remote_copy(
            src_ref=src,
            dst_ref=dst,
            send_sem=send_sems.at[stage, d],
            recv_sem=recv_sems.at[stage, d],
            device_id=device((mine + d) % size),
            device_id_type=MESH,
        )

    def each(axis, step):
        def body(d, carry):
            step(d)
            return carry

        lax.fori_loop(1, axis[0], body, 0)

    def send_all(stage, axis, src_of, buffer):
        size, mine, _ = axis

        def step(d):
            copy_to(stage, axis, d, src_of((mine + d) % size), buffer.at[mine]).start()

        each(axis, step)

    def wait_from(stage, axis, d, buffer):
        size, mine, _ = axis
        slot = buffer.at[(mine + size - d) % size]
        copy_to(stage, axis, d, slot, slot).wait_recv()

    def wait_all(stage, axis, buffer):
        each(axis, lambda d: wait_from(stage, axis, d, buffer))

    def sent_all(stage, axis, src_of, buffer):
        size, mine, _ = axis

        def step(d):
            copy_to(stage, axis, d, src_of((mine + d) % size), buffer.at[mine]).wait_send()

        each(axis, step)

    def total(buffer, size):
        result = buffer[0]
        for p in range(1, size):
            result = result + buffer[p]
        return result

    barrier = pltpu.get_barrier_semaphore()
    for axis in (along_z, along_q, along_r):
        size, mine, device = axis

        def greet(d, size=size, mine=mine, device=device):
            pl.semaphore_signal(
                barrier, inc=1, device_id=device((mine + d) % size), device_id_type=MESH
            )

        each(axis, greet)

    mm_all[z, 0:3, :] = mm_ref[...]
    mm_all[z, 3:4, :] = charge_ref[...]
    live_row = lax.broadcasted_iota(jnp.int32, (1, atoms), 1) < count_ref[...]
    qm_all[q, 0:3, :] = qm_ref[...]
    qm_all[q, 3:4, :] = jnp.where(live_row, species_ref[...], -1).astype(F32)

    pl.semaphore_wait(barrier, nz + nq + nr - 3)
    send_all(QM_Q, along_q, lambda p: qm_all.at[q], qm_all)
    send_all(MM_Z, along_z, lambda p: mm_all.at[z], mm_all)

    table_wide[...] = jnp.zeros_like(table_wide)
    table_wide[0 : table_ref.shape[0], :] = table_ref[...].astype(F32)
    lane = lax.broadcasted_iota(jnp.int32, (atoms, LANES), 1)
    row = lax.broadcasted_iota(jnp.int32, (atoms, LANES), 0)
    for k in range(neighbours + 1):
        rows = slice(k * atoms, (k + 1) * atoms)
        if k < neighbours:
            hot = (lane == owner_ref[:, k : k + 1]).astype(F32)
            slots = (lane == slot_ref[:, k : k + 1]).astype(F32)
        else:
            hot = (lane == blk).astype(F32)
            slots = (lane == row).astype(F32)
        owner_hot[rows, :] = hot.astype(BF16)
        owner_hot_t[:, rows] = jnp.transpose(hot)[0 : owner_hot_t.shape[0], :].astype(BF16)
        slot_hot[rows, :] = slots
    acc_x[...] = jnp.zeros_like(acc_x)

    def wide(line):
        return jnp.transpose(jnp.broadcast_to(line, (LANES, atoms)))

    wait_all(QM_Q, along_q, qm_all)

    def widen(p, carry):
        rows = pl.ds(pl.multiple_of(p * atoms, atoms), atoms)
        wide_x[rows, :] = wide(qm_all[p, 0:1, :])
        wide_y[rows, :] = wide(qm_all[p, 1:2, :])
        wide_z[rows, :] = wide(qm_all[p, 2:3, :])
        pot_z[z, pl.ds(nq + p, 1), :] = qm_all[p, 3:4, :]
        return carry

    lax.fori_loop(0, nq, widen, 0)

    def columns(chunk):
        return [
            [mm_all[chunk, c : c + 1, t * LANES : (t + 1) * LANES] for c in range(4)]
            for t in range(mm_tiles)
        ]

    def potential_chunk(d, carry):
        @pl.when(d > 0)
        def _():
            wait_from(MM_Z, along_z, d, mm_all)

        tiles = columns((z + nz - d) % nz)

        def group(g, inner):
            rows = pl.ds(pl.multiple_of(g * POT_ROWS, POT_ROWS), POT_ROWS)
            x, y, w = wide_x[rows, :], wide_y[rows, :], wide_z[rows, :]
            running = acc_x[rows, :]
            for mx, my, mz, mq in tiles:
                dx, dy, dz = x - mx, y - my, w - mz
                inverse = lax.rsqrt(dx * dx + dy * dy + (dz * dz + SOFTEN))
                running = running + inverse * mq
            acc_x[rows, :] = running
            return inner

        return lax.fori_loop(0, nq * atoms // POT_ROWS, group, carry)

    lax.fori_loop(0, nz, potential_chunk, 0)

    def lines(acc, p):
        rows = pl.ds(pl.multiple_of(p * atoms, atoms), atoms)
        return jnp.sum(jnp.transpose(acc[rows, :]), axis=0, keepdims=True)

    def gather_potential(p, carry):
        pot_q[q, pl.ds(p, 1), :] = lines(acc_x, p)
        return carry

    lax.fori_loop(0, nq, gather_potential, 0)
    send_all(POT_Q, along_q, lambda p: pot_q.at[q], pot_q)
    wait_all(POT_Q, along_q, pot_q)
    pot_r[rep] = total(pot_q, nq)
    send_all(POT_R, along_r, lambda p: pot_r.at[rep], pot_r)
    wait_all(POT_R, along_r, pot_r)
    pot_z[z, 0:nq, :] = total(pot_r, nr) * coupling
    send_all(POT_Z, along_z, lambda p: pot_z.at[z], pot_z)
    acc_x[...] = jnp.zeros_like(acc_x)
    acc_y[...] = jnp.zeros_like(acc_y)
    acc_z[...] = jnp.zeros_like(acc_z)
    wait_all(POT_Z, along_z, pot_z)

    potentials = jnp.concatenate([pot_z[p, 0:nq, :] for p in range(nz)], axis=0)
    codes = jnp.concatenate([pot_z[p, nq : 2 * nq, :] for p in range(nz)], axis=0)
    gain = gain_ref[...]
    table = table_wide[...].astype(BF16)
    pieces = [*split3(potentials), codes.astype(BF16)]
    neighbour = jnp.zeros((atoms, LANES), F32)
    for k in range(neighbours + 1):
        rows = slice(k * atoms, (k + 1) * atoms)
        hot = owner_hot[rows, 0:blocks]
        slots = slot_hot[rows, :]
        picked = [jnp.dot(hot, piece, preferred_element_type=F32) for piece in pieces]
        potential = jnp.sum((picked[0] + picked[1] + picked[2]) * slots, axis=1, keepdims=True)
        code = jnp.sum(picked[3] * slots, axis=1, keepdims=True)
        live = (code >= 0).astype(F32)
        kinds = (lane.astype(F32) == code).astype(F32).astype(BF16)
        base = jnp.dot(kinds, table, preferred_element_type=F32)
        start = (live * (base + potential * gain)).astype(BF16)
        if k < neighbours:
            neighbour = neighbour + start.astype(F32)
    mixed = start.astype(F32) + jnp.dot(
        neighbour.astype(BF16), message_ref[...], preferred_element_type=F32
    )
    before = jnp.dot(mixed.astype(BF16), hidden_ref[...], preferred_element_type=F32)
    sigma = jax.nn.sigmoid(before)
    active = before * sigma
    charge_part = live * jnp.sum(active * readout_ref[...], axis=1, keepdims=True)
    back_active = live * (energy_ref[...] + potential * readout_ref[...])
    back_before = (back_active * sigma * (1.0 + before * (1.0 - sigma))).astype(BF16)
    nt = (((1,), (1,)), ((), ()))
    back_mixed = lax.dot_general(back_before, hidden_ref[...], nt, preferred_element_type=F32)
    back_sum = lax.dot_general(
        back_mixed.astype(BF16), message_ref[...], nt, preferred_element_type=F32
    ).astype(BF16)
    out_going = jnp.sum(back_sum.astype(F32) * gain, axis=1, keepdims=True)
    staying = jnp.sum(back_mixed * gain, axis=1, keepdims=True) + charge_part
    spread = jnp.zeros((blocks, LANES), F32)
    parts_out, parts_stay = split3(out_going), split3(staying)
    for k in range(neighbours + 1):
        rows = slice(k * atoms, (k + 1) * atoms)
        slots = slot_hot[rows, :]
        for part in parts_out if k < neighbours else parts_stay:
            spread = spread + jnp.dot(
                owner_hot_t[0:blocks, rows],
                (slots * part.astype(F32)).astype(BF16),
                preferred_element_type=F32,
            )
    for p in range(nz):
        grad_mine[p] = spread[p * nq : (p + 1) * nq, :]
    send_all(GRAD_Z, along_z, lambda p: grad_mine.at[p], grad_z)
    grad_z[z] = grad_mine[z]
    energy_part = live * jnp.sum(active * energy_ref[...], axis=1, keepdims=True)
    atom_energy = energy_part + charge_part * potential
    atom_energy_ref[...] = jnp.sum(
        jnp.where(lane == row, atom_energy, 0.0), axis=0, keepdims=True
    )
    wait_all(GRAD_Z, along_z, grad_z)
    grad_q[q] = total(grad_z, nz)
    send_all(GRAD_Q, along_q, lambda p: grad_q.at[q], grad_q)
    wait_all(GRAD_Q, along_q, grad_q)
    live_plane = (pot_z[z, nq : 2 * nq, :] >= 0).astype(F32)
    grad_sum[...] = live_plane * total(grad_q, nq)

    def widen_effective(p, carry):
        rows = pl.ds(pl.multiple_of(p * atoms, atoms), atoms)
        wide_e[rows, :] = wide(grad_sum[pl.ds(p, 1), :])
        return carry

    lax.fori_loop(0, nq, widen_effective, 0)

    def force_chunk(d, carry):
        chunk = (z + d) % nz
        tiles = columns(chunk)

        def group(g, mm_running):
            rows = pl.ds(pl.multiple_of(g * FORCE_ROWS, FORCE_ROWS), FORCE_ROWS)
            x, y, w, e = wide_x[rows, :], wide_y[rows, :], wide_z[rows, :], wide_e[rows, :]
            fx, fy, fz = acc_x[rows, :], acc_y[rows, :], acc_z[rows, :]
            mm_next = []
            for t, (mx, my, mz, mq) in enumerate(tiles):
                dx, dy, dz = x - mx, y - my, w - mz
                inverse = lax.rsqrt(dx * dx + dy * dy + (dz * dz + SOFTEN))
                cube = inverse * inverse * inverse
                on_qm = cube * mq
                on_mm = cube * e
                fx, fy, fz = fx + on_qm * dx, fy + on_qm * dy, fz + on_qm * dz
                for c, offset in enumerate((dx, dy, dz)):
                    term = jnp.sum((on_mm * offset).reshape(FORCE_ROWS // 8, 8, LANES), axis=0)
                    mm_next.append(mm_running[3 * t + c] + term)
            acc_x[rows, :], acc_y[rows, :], acc_z[rows, :] = fx, fy, fz
            return tuple(mm_next)

        nothing = tuple(jnp.zeros((8, LANES), F32) for _ in range(3 * mm_tiles))
        sums = lax.fori_loop(0, nq * atoms // FORCE_ROWS, group, nothing)
        for t in range(mm_tiles):
            for c in range(3):
                mmf_mine[chunk, c : c + 1, t * LANES : (t + 1) * LANES] = jnp.sum(
                    sums[3 * t + c], axis=0, keepdims=True
                )

        @pl.when(d < nz)
        def _():
            copy_to(MMF_Z, along_z, d, mmf_mine.at[chunk], mmf_z.at[z]).start()

        return carry

    lax.fori_loop(1, nz + 1, force_chunk, 0)
    mmf_z[z] = mmf_mine[z]

    def gather_force(p, carry):
        qmf_mine[p, 0:1, :] = lines(acc_x, p)
        qmf_mine[p, 1:2, :] = lines(acc_y, p)
        qmf_mine[p, 2:3, :] = lines(acc_z, p)
        return carry

    lax.fori_loop(0, nq, gather_force, 0)
    send_all(QMF_Q, along_q, lambda p: qmf_mine.at[p], qmf_q)
    qmf_q[q] = qmf_mine[q]
    wait_all(MMF_Z, along_z, mmf_z)
    mm_force_ref[...] = total(mmf_z, nz) * (charge_ref[...] * -coupling)
    wait_all(QMF_Q, along_q, qmf_q)
    qmf_r[rep] = total(qmf_q, nq)
    send_all(QMF_R, along_r, lambda p: qmf_r.at[rep], qmf_r)
    sent_all(QM_Q, along_q, lambda p: qm_all.at[q], qm_all)
    sent_all(MM_Z, along_z, lambda p: mm_all.at[z], mm_all)
    sent_all(POT_Q, along_q, lambda p: pot_q.at[q], pot_q)
    sent_all(POT_R, along_r, lambda p: pot_r.at[rep], pot_r)
    sent_all(POT_Z, along_z, lambda p: pot_z.at[z], pot_z)
    sent_all(GRAD_Z, along_z, lambda p: grad_mine.at[p], grad_z)
    sent_all(GRAD_Q, along_q, lambda p: grad_q.at[q], grad_q)
    sent_all(MMF_Z, along_z, lambda p: mmf_mine.at[p], mmf_z)
    sent_all(QMF_Q, along_q, lambda p: qmf_mine.at[p], qmf_q)
    wait_all(QMF_R, along_r, qmf_r)
    qm_force_ref[...] = total(qmf_r, nr) * (grad_sum[pl.ds(q, 1), :] * coupling)
    sent_all(QMF_R, along_r, lambda p: qmf_r.at[rep], qmf_r)


def on_device(
    nz,
    nq,
    nr,
    qm_pos,
    species,
    qm_count,
    ghost_owner,
    ghost_slot,
    mm_pos,
    mm_charge,
    species_table,
    potential_gain,
    message_weight,
    hidden_weight,
    energy_readout,
    charge_readout,
):
    atoms = qm_pos.shape[1]
    mm_here = mm_pos.shape[1]
    coupling = float(mm_here * nz * nq * nr) ** (-0.5)
    plane = nq * atoms
    slots = max(nz, nq, nr)
    groups = ghost_owner.shape[1] + 1
    hot_rows = -(-nz * nq // 16) * 16
    small = lambda *shape: pltpu.VMEM(shape, F32)
    vmem = pl.BlockSpec(memory_space=pltpu.VMEM)
    atom_energy, qm_force, mm_force = pl.pallas_call(
        functools.partial(kernel, nz, nq, nr, coupling),
        out_shape=(
            jax.ShapeDtypeStruct((1, atoms), F32),
            jax.ShapeDtypeStruct((3, atoms), F32),
            jax.ShapeDtypeStruct((3, mm_here), F32),
        ),
        in_specs=[vmem] * 13,
        out_specs=(vmem,) * 3,
        scratch_shapes=[
            small(nz, 4, mm_here),
            small(nq, 4, atoms),
            small(nq, nq, atoms),
            small(nr, nq, atoms),
            small(nz, 2 * nq, atoms),
            small(nz, nq, atoms),
            small(nz, nq, atoms),
            small(nq, atoms),
            small(nq, nq, atoms),
            small(nz, 3, mm_here),
            small(nz, 3, mm_here),
            small(nq, 3, atoms),
            small(nq, 3, atoms),
            small(nr, 3, atoms),
            small(plane, LANES),
            small(plane, LANES),
            small(plane, LANES),
            small(plane, LANES),
            small(plane, LANES),
            small(plane, LANES),
            small(plane, LANES),
            small(LANES, LANES),
            pltpu.VMEM((groups * atoms, LANES), BF16),
            pltpu.VMEM((hot_rows, groups * atoms), BF16),
            small(groups * atoms, LANES),
            pltpu.SemaphoreType.DMA((10, slots)),
            pltpu.SemaphoreType.DMA((10, slots)),
        ],
        compiler_params=pltpu.CompilerParams(
            collective_id=0, has_side_effects=True, vmem_limit_bytes=40 * 2**20
        ),
    )(
        qm_pos,
        species[None, :],
        qm_count[None, :],
        ghost_owner,
        ghost_slot,
        mm_pos,
        mm_charge[None, :],
        species_table,
        potential_gain[None, :],
        message_weight,
        hidden_weight,
        energy_readout[None, :],
        charge_readout[None, :],
    )
    return (atom_energy[0], qm_force, mm_force)


def solution(mesh):
    blocks, nr = mesh.shape["blk"], mesh.shape["rep"]
    nq = min(8, blocks // 2)
    placed = (
        P(None, "blk"),
        P("blk"),
        P("blk"),
        P("blk", None),
        P("blk", None),
        P(None, ("blk", "rep")),
        P(("blk", "rep")),
        P(),
        P(),
        P(),
        P(),
        P(),
        P(),
    )
    return jax.shard_map(
        functools.partial(on_device, blocks // nq, nq, nr),
        mesh=mesh,
        in_specs=placed,
        out_specs=(P("blk"), P(None, "blk"), P(None, ("blk", "rep"))),
        check_vma=False,
    )
```

time: 972 us -> 101 us (0.10)
  waiting for transfers between devices: 438 us -> 0 us
  blocking collectives: 346 us -> 0 us
  Pallas kernels: 0 us -> 95.4 us
  local copies, waits for them, and re-layouts: 93 us -> 3.78 us
  other arithmetic: 46.4 us -> 0 us
  starting transfers between devices: 23.2 us -> 0 us
  between operations: 15 us -> 1.38 us
    unnamed x2 -> x0, waiting for transfers between devices: 420 us -> none
    all_gather x2 -> x0, blocking collectives: 240 us -> none  [the longest x1 124 us: on_device(): lax.all_gather(mm_stack, 'blk', axis=1, tiled=True)]
    pallas_call x0 -> x1, Pallas kernels: none -> 95.4 us  [on_device(): pl.pallas_call(functools.partial(kernel, nz, nq, nr, coupling), out_shape...]
    psum x2 -> x0, blocking collectives: 79.1 us -> none  [the longest x1 40.8 us: on_device(): qm_force = lax.psum(block_force, 'rep') * coupling]
    scatter x2 -> x0, local copies, waits for them, and re-layouts: 76.6 us -> none  [the longest x1 51.5 us: on_device(): outgoing_grads = jnp.zeros((blocks, capacity, channels), jnp.bfloat16).at...]
    reduce_sum x162 -> x0, other arithmetic: 37.6 us -> none  [the longest x80 14.7 us: pair_parts(): inverse = lax.rsqrt(jnp.sum(offset * offset, axis=0) + SOFTEN)]
    all_to_all x1 -> x0, blocking collectives: 27.1 us -> none  [on_device(): lax.all_to_all(outgoing, 'blk', split_axis=0, concat_axis=0, tiled=True)]
    all_to_all x2 -> x0, starting transfers between devices: 23.2 us -> none  [the longest x1 17.2 us: on_device(): lax.all_to_all(request, 'blk', split_axis=0, concat_axis=0, tiled=True)]
  transfers between devices with their start and end apart: 3 -> 0, of which waited for: 2 -> 0; matrix products, arithmetic and copies ran while one was open for 2% -> 0% of each run, Pallas kernels for 0% -> 0%
where the time goes in v1:
time: 101 us
  Pallas kernels  95.4 us (94%)
  local copies, waits for them, and re-layouts  3.78 us (4%)
  between operations  1.38 us (1%)
    pallas_call x1, Pallas kernels, on_device(): pl.pallas_call(functools.partial(kernel, nz, nq, nr, coupling), out_shape...  95.4 us
    unnamed x29, local copies, waits for them, and re-layouts  3.78 us

profile of v1, /device:TPU:1, one launch (start us, length us, event | category | flops | bytes accessed | tf_op | source)
XLA Modules:
  0.0 100.6 jit_solution(650368191975239449)
XLA Ops:
  1.3 0.0 copy-start.10
  1.3 0.7 copy-done.10
  2.0 0.0 copy-start.11
  2.0 0.0 copy-start
  2.0 0.1 copy.16.owner_ref
  2.1 0.6 copy-done.11
  2.6 0.0 copy-start.1
  2.6 0.0 copy-start.2
  2.6 0.0 copy-start.3
  2.6 0.0 copy-start.4
  2.7 0.0 copy-start.5
  2.7 0.0 copy-start.6
  2.7 0.0 copy-start.7
  2.7 0.0 copy-start.8
  2.7 0.0 copy-start.9
  2.7 0.1 copy.17.slot_ref
  2.8 0.0 copy-done
  2.8 0.6 copy-done.1
  3.4 0.0 copy-done.2
  3.4 0.0 copy-done.3
  3.4 0.0 copy-done.4
  3.4 0.0 copy-done.5
  3.4 0.0 copy-done.6
  3.4 0.0 copy-done.7
  3.4 0.0 copy-done.8
  3.5 0.0 copy-done.9
  3.5 95.4 %shard_map.148 = (f32[1,128]{1,0:T(1,128)S(1)}, f32[3,128]{1,0:T(4,128)S(1)}, f32[3,512]{1,0:T(4,128)S(1)}) custom-call(f32[3,128]{1,0:T(4,128)S(1)} %copy-done.3, s32[1,128]{1,0:T(1,128)S(1)} %bitcast.11, s32[1,1]{1,0:T(1,128)} %bitcast.7.count_ref, s32[128,4]{1,0:T(8,128)S(1)} %copy.16.owner_ref, s32[128,4]{1,0:T(8,128)S(1)} %copy.17.slot_ref, ...), custom_call_target="tpu_custom_call" | custom-call | tf_op jit(solution)/shard_map/pallas_call | solution.py:404
  98.9 0.5 copy.22
  99.4 0.6 copy.23
  100.0 0.6 copy.24
Async XLA Ops:
  1.3 0.7 copy-start.10
  2.0 0.7 copy-start.11
  2.0 0.9 copy-start
  2.6 0.8 copy-start.1
  2.6 0.8 copy-start.2
  2.6 0.8 copy-start.3
  2.6 0.8 copy-start.4
  2.7 0.8 copy-start.5
  2.7 0.8 copy-start.6
  2.7 0.8 copy-start.7
  2.7 0.8 copy-start.8
  2.7 0.8 copy-start.9

commit v2 on v1

v2 whole, which is shorter than its diff:
```python
import functools

import jax
import jax.numpy as jnp
from jax import lax
from jax.experimental import pallas as pl
from jax.experimental.pallas import tpu as pltpu
from jax.sharding import PartitionSpec as P

SOFTEN = 0.25
LANES = 128
POT_ROWS = 64
FORCE_ROWS = 32
EARLY = 2
MESH = pl.DeviceIdType.MESH
F32 = jnp.float32
BF16 = jnp.bfloat16

QM_N, MM_Q, POT_X, POT_Z, POT_Q, GRAD_Q, GRAD_N, QMF_Z, QMF_X, MMF_Q = range(10)


def split3(value):
    high = value.astype(BF16)
    rest = value - high.astype(F32)
    middle = rest.astype(BF16)
    low = (rest - middle.astype(F32)).astype(BF16)
    return high, middle, low


def kernel(
    nz,
    nq,
    nx,
    coupling,
    qm_ref,
    species_ref,
    count_ref,
    owner_ref,
    slot_ref,
    mm_ref,
    charge_ref,
    table_ref,
    gain_ref,
    message_ref,
    hidden_ref,
    energy_ref,
    readout_ref,
    atom_energy_ref,
    qm_force_ref,
    mm_force_ref,
    mm_all,
    qm_all,
    pot_x,
    pot_z,
    pot_q,
    grad_mine,
    grad_q,
    grad_n,
    grad_sum,
    qmf_mine,
    qmf_z,
    qmf_x,
    mmf_mine,
    mmf_q,
    wide_x,
    wide_y,
    wide_z,
    wide_e,
    wide_ex,
    wide_ey,
    wide_ez,
    acc_x,
    acc_y,
    acc_z,
    inverses,
    table_wide,
    owner_hot,
    owner_hot_t,
    slot_hot,
    send_sems,
    recv_sems,
):
    blk = lax.axis_index("blk")
    rep = lax.axis_index("rep")
    z, q = blk // nq, blk % nq
    x, ring = rep // 2, (rep % 2) * nz + z
    rings = 2 * nz
    atoms = qm_ref.shape[1]
    mm_tiles = mm_ref.shape[1] // LANES
    blocks = nz * nq
    neighbours = owner_ref.shape[1]

    def at_ring(p):
        return ((p % nz) * nq + q, x * 2 + p // nz)

    def at_q(p):
        return (z * nq + p, rep)

    def shift(d):
        return jnp.where(d < nz // 2, d, d - nz)

    def q_place(d, sign):
        y = (q // 2 + (nq // 2) + sign * (d // 2)) % (nq // 2)
        return y * 2 + (q + d) % 2

    same = lambda p: p
    near = (nz, ring, lambda d: (ring + rings - shift(d)) % rings, lambda d: (ring + rings + shift(d)) % rings, at_ring, lambda p: p % nz)
    far = (rings, ring, lambda d: (ring + d) % rings, lambda d: (ring + rings - d) % rings, at_ring, same)
    plane = (nq, q, lambda d: q_place(d, 1), lambda d: q_place(d, -1), at_q, same)
    row_x = (nx, x, lambda d: (x + d) % nx, lambda d: (x + nx - d) % nx, lambda p: (blk, p * 2 + rep % 2), same)

    def copy_to(stage, d, device, src, dst):
        return pltpu.make_async_remote_copy(
            src_ref=src,
            dst_ref=dst,
            send_sem=send_sems.at[stage, d],
            recv_sem=recv_sems.at[stage, d],
            device_id=device,
            device_id_type=MESH,
        )

    def each(axis, step):
        def body(d, carry):
            step(d)
            return carry

        lax.fori_loop(1, axis[0], body, 0)

    def outgoing(stage, axis, src_of, buffer, d):
        _, mine, to, _, device, slot = axis
        p = to(d)
        return copy_to(stage, d, device(p), src_of(p), buffer.at[slot(mine)])

    def send_all(stage, axis, src_of, buffer):
        each(axis, lambda d: outgoing(stage, axis, src_of, buffer, d).start())

    def sent_all(stage, axis, src_of, buffer):
        each(axis, lambda d: outgoing(stage, axis, src_of, buffer, d).wait_send())

    def wait_from(stage, axis, d, buffer):
        _, _, _, came, device, slot = axis
        p = came(d)
        place = buffer.at[slot(p)]
        copy_to(stage, d, device(p), place, place).wait_recv()
        return slot(p)

    def wait_all(stage, axis, buffer):
        def step(d):
            wait_from(stage, axis, d, buffer)

        each(axis, step)

    def total(buffer, size):
        result = buffer[0]
        for p in range(1, size):
            result = result + buffer[p]
        return result

    barrier = pltpu.get_barrier_semaphore()
    for axis in (far, plane, row_x):

        def greet(d, axis=axis):
            pl.semaphore_signal(barrier, inc=1, device_id=axis[4](axis[2](d)), device_id_type=MESH)

        each(axis, greet)

    mm_all[q, 0:3, :] = mm_ref[...]
    mm_all[q, 3:4, :] = charge_ref[...]
    live_row = lax.broadcasted_iota(jnp.int32, (1, atoms), 1) < count_ref[...]
    qm_all[z, 0:3, :] = qm_ref[...]
    qm_all[z, 3:4, :] = jnp.where(live_row, species_ref[...], -1).astype(F32)

    pl.semaphore_wait(barrier, rings + nq + nx - 3)
    send_all(QM_N, near, lambda p: qm_all.at[z], qm_all)
    send_all(MM_Q, plane, lambda p: mm_all.at[q], mm_all)

    table_wide[...] = jnp.zeros_like(table_wide)
    table_wide[0 : table_ref.shape[0], :] = table_ref[...].astype(F32)
    lane = lax.broadcasted_iota(jnp.int32, (atoms, LANES), 1)
    row = lax.broadcasted_iota(jnp.int32, (atoms, LANES), 0)
    for k in range(neighbours + 1):
        rows = slice(k * atoms, (k + 1) * atoms)
        if k < neighbours:
            owner = owner_ref[:, k : k + 1]
            hot = (lane == (owner % nq) * nz + owner // nq).astype(F32)
            slots = (lane == slot_ref[:, k : k + 1]).astype(F32)
        else:
            hot = (lane == q * nz + z).astype(F32)
            slots = (lane == row).astype(F32)
        owner_hot[rows, :] = hot.astype(BF16)
        owner_hot_t[:, rows] = jnp.transpose(hot)[0 : owner_hot_t.shape[0], :].astype(BF16)
        slot_hot[rows, :] = slots
    acc_x[...] = jnp.zeros_like(acc_x)

    def wide(line):
        return jnp.transpose(jnp.broadcast_to(line, (LANES, atoms)))

    def block_rows(p):
        return pl.ds(pl.multiple_of(p * atoms, atoms), atoms)

    def widen(p):
        rows = block_rows(p)
        wide_x[rows, :] = wide(qm_all[p, 0:1, :])
        wide_y[rows, :] = wide(qm_all[p, 1:2, :])
        wide_z[rows, :] = wide(qm_all[p, 2:3, :])
        pot_q[q, pl.ds(nz + p, 1), :] = qm_all[p, 3:4, :]

    widen(z)
    each(near, lambda d: widen(wait_from(QM_N, near, d, qm_all)))

    def columns(chunk):
        return [
            [mm_all[chunk, c : c + 1, t * LANES : (t + 1) * LANES] for c in range(4)]
            for t in range(mm_tiles)
        ]

    def potential_chunk(d, carry):
        @pl.when(d > 0)
        def _():
            wait_from(MM_Q, plane, d, mm_all)

        chunk = plane[3](d)
        tiles = columns(chunk)

        def group(g, inner):
            rows = pl.ds(pl.multiple_of(g * POT_ROWS, POT_ROWS), POT_ROWS)
            px, py, pz = wide_x[rows, :], wide_y[rows, :], wide_z[rows, :]
            running = acc_x[rows, :]
            for t, (mx, my, mz, mq) in enumerate(tiles):
                dx, dy, dz = px - mx, py - my, pz - mz
                inverse = lax.rsqrt(dx * dx + dy * dy + (dz * dz + SOFTEN))
                inverses[chunk, rows, t * LANES : (t + 1) * LANES] = inverse
                running = running + inverse * mq
            acc_x[rows, :] = running
            return inner

        return lax.fori_loop(0, nz * atoms // POT_ROWS, group, carry)

    lax.fori_loop(0, nq, potential_chunk, 0)

    def lines(acc, p):
        return jnp.sum(jnp.transpose(acc[block_rows(p), :]), axis=0, keepdims=True)

    def gather_potential(p, carry):
        pot_x[x, pl.ds(p, 1), :] = lines(acc_x, p)
        return carry

    lax.fori_loop(0, nz, gather_potential, 0)
    send_all(POT_X, row_x, lambda p: pot_x.at[x], pot_x)
    acc_x[...] = jnp.zeros_like(acc_x)
    acc_y[...] = jnp.zeros_like(acc_y)
    acc_z[...] = jnp.zeros_like(acc_z)

    def pull_chunk(chunk, carry):
        tiles = columns(chunk)

        def group(g, inner):
            rows = pl.ds(pl.multiple_of(g * FORCE_ROWS, FORCE_ROWS), FORCE_ROWS)
            px, py, pz = wide_x[rows, :], wide_y[rows, :], wide_z[rows, :]
            fx, fy, fz = acc_x[rows, :], acc_y[rows, :], acc_z[rows, :]
            for t, (mx, my, mz, mq) in enumerate(tiles):
                where = slice(t * LANES, (t + 1) * LANES)
                inverse = inverses[chunk, rows, where]
                cube = inverse * inverse * inverse
                inverses[chunk, rows, where] = cube
                pull = cube * mq
                fx = fx + pull * (px - mx)
                fy = fy + pull * (py - my)
                fz = fz + pull * (pz - mz)
            acc_x[rows, :], acc_y[rows, :], acc_z[rows, :] = fx, fy, fz
            return inner

        return lax.fori_loop(0, nz * atoms // FORCE_ROWS, group, carry)

    early = min(EARLY, nq)
    lax.fori_loop(0, early, pull_chunk, 0)
    wait_all(POT_X, row_x, pot_x)
    pot_z[ring] = total(pot_x, nx)
    send_all(POT_Z, far, lambda p: pot_z.at[ring], pot_z)
    lax.fori_loop(early, nq, pull_chunk, 0)

    def gather_force(p, carry):
        qmf_mine[p, 0:1, :] = lines(acc_x, p)
        qmf_mine[p, 1:2, :] = lines(acc_y, p)
        qmf_mine[p, 2:3, :] = lines(acc_z, p)
        return carry

    lax.fori_loop(0, nz, gather_force, 0)
    qmf_z[ring] = qmf_mine[z]
    wait_all(POT_Z, far, pot_z)
    pot_q[q, 0:nz, :] = total(pot_z, rings) * coupling
    send_all(POT_Q, plane, lambda p: pot_q.at[q], pot_q)
    send_all(QMF_Z, far, lambda p: qmf_mine.at[p % nz], qmf_z)
    wait_all(POT_Q, plane, pot_q)

    potentials = jnp.concatenate([pot_q[p, 0:nz, :] for p in range(nq)], axis=0)
    codes = jnp.concatenate([pot_q[p, nz : 2 * nz, :] for p in range(nq)], axis=0)
    gain = gain_ref[...]
    table = table_wide[...].astype(BF16)
    pieces = [*split3(potentials), codes.astype(BF16)]
    neighbour = jnp.zeros((atoms, LANES), F32)
    for k in range(neighbours + 1):
        rows = slice(k * atoms, (k + 1) * atoms)
        hot = owner_hot[rows, 0:blocks]
        slots = slot_hot[rows, :]
        picked = [jnp.dot(hot, piece, preferred_element_type=F32) for piece in pieces]
        potential = jnp.sum((picked[0] + picked[1] + picked[2]) * slots, axis=1, keepdims=True)
        code = jnp.sum(picked[3] * slots, axis=1, keepdims=True)
        live = (code >= 0).astype(F32)
        kinds = (lane.astype(F32) == code).astype(F32).astype(BF16)
        base = jnp.dot(kinds, table, preferred_element_type=F32)
        start = (live * (base + potential * gain)).astype(BF16)
        if k < neighbours:
            neighbour = neighbour + start.astype(F32)
    mixed = start.astype(F32) + jnp.dot(
        neighbour.astype(BF16), message_ref[...], preferred_element_type=F32
    )
    before = jnp.dot(mixed.astype(BF16), hidden_ref[...], preferred_element_type=F32)
    sigma = jax.nn.sigmoid(before)
    active = before * sigma
    charge_part = live * jnp.sum(active * readout_ref[...], axis=1, keepdims=True)
    back_active = live * (energy_ref[...] + potential * readout_ref[...])
    back_before = (back_active * sigma * (1.0 + before * (1.0 - sigma))).astype(BF16)
    nt = (((1,), (1,)), ((), ()))
    back_mixed = lax.dot_general(back_before, hidden_ref[...], nt, preferred_element_type=F32)
    back_sum = lax.dot_general(
        back_mixed.astype(BF16), message_ref[...], nt, preferred_element_type=F32
    ).astype(BF16)
    out_going = jnp.sum(back_sum.astype(F32) * gain, axis=1, keepdims=True)
    staying = jnp.sum(back_mixed * gain, axis=1, keepdims=True) + charge_part
    spread = jnp.zeros((blocks, LANES), F32)
    parts_out, parts_stay = split3(out_going), split3(staying)
    for k in range(neighbours + 1):
        rows = slice(k * atoms, (k + 1) * atoms)
        slots = slot_hot[rows, :]
        for part in parts_out if k < neighbours else parts_stay:
            spread = spread + jnp.dot(
                owner_hot_t[0:blocks, rows],
                (slots * part.astype(F32)).astype(BF16),
                preferred_element_type=F32,
            )
    for p in range(nq):
        grad_mine[p] = spread[p * nz : (p + 1) * nz, :]
    send_all(GRAD_Q, plane, lambda p: grad_mine.at[p], grad_q)
    grad_q[q] = grad_mine[q]
    energy_part = live * jnp.sum(active * energy_ref[...], axis=1, keepdims=True)
    atom_energy = energy_part + charge_part * potential
    atom_energy_ref[...] = jnp.sum(
        jnp.where(lane == row, atom_energy, 0.0), axis=0, keepdims=True
    )
    wait_all(GRAD_Q, plane, grad_q)
    grad_n[z] = total(grad_q, nq)
    send_all(GRAD_N, near, lambda p: grad_n.at[z], grad_n)
    wait_all(QMF_Z, far, qmf_z)
    qmf_x[x] = total(qmf_z, rings)
    send_all(QMF_X, row_x, lambda p: qmf_x.at[x], qmf_x)
    wait_all(GRAD_N, near, grad_n)
    live_plane = (pot_q[q, nz : 2 * nz, :] >= 0).astype(F32)
    grad_sum[...] = live_plane * total(grad_n, nz)

    def widen_effective(p, carry):
        rows = block_rows(p)
        effective = wide(grad_sum[pl.ds(p, 1), :])
        wide_e[rows, :] = effective
        wide_ex[rows, :] = effective * wide_x[rows, :]
        wide_ey[rows, :] = effective * wide_y[rows, :]
        wide_ez[rows, :] = effective * wide_z[rows, :]
        return carry

    lax.fori_loop(0, nz, widen_effective, 0)

    def push_chunk(step, carry):
        d = nq - step
        chunk = jnp.where(d > 0, plane[2](d), q)

        def group(g, running):
            rows = pl.ds(pl.multiple_of(g * FORCE_ROWS, FORCE_ROWS), FORCE_ROWS)
            weights = wide_e[rows, :], wide_ex[rows, :], wide_ey[rows, :], wide_ez[rows, :]
            after = []
            for t in range(mm_tiles):
                cube = inverses[chunk, rows, t * LANES : (t + 1) * LANES]
                for c, weight in enumerate(weights):
                    term = jnp.sum((cube * weight).reshape(FORCE_ROWS // 8, 8, LANES), axis=0)
                    after.append(running[4 * t + c] + term)
            return tuple(after)

        nothing = tuple(jnp.zeros((8, LANES), F32) for _ in range(4 * mm_tiles))
        sums = lax.fori_loop(0, nz * atoms // FORCE_ROWS, group, nothing)
        for t in range(mm_tiles):
            where = slice(t * LANES, (t + 1) * LANES)
            plain, *moments = [jnp.sum(sums[4 * t + c], axis=0, keepdims=True) for c in range(4)]
            for c in range(3):
                mmf_mine[chunk, c : c + 1, where] = moments[c] - plain * mm_all[chunk, c : c + 1, where]

        @pl.when(d > 0)
        def _():
            outgoing(MMF_Q, plane, lambda p: mmf_mine.at[p], mmf_q, d).start()

        return carry

    lax.fori_loop(1, nq + 1, push_chunk, 0)
    mmf_q[q] = mmf_mine[q]
    sent_all(QM_N, near, lambda p: qm_all.at[z], qm_all)
    sent_all(MM_Q, plane, lambda p: mm_all.at[q], mm_all)
    sent_all(POT_X, row_x, lambda p: pot_x.at[x], pot_x)
    sent_all(POT_Z, far, lambda p: pot_z.at[ring], pot_z)
    sent_all(POT_Q, plane, lambda p: pot_q.at[q], pot_q)
    sent_all(QMF_Z, far, lambda p: qmf_mine.at[p % nz], qmf_z)
    sent_all(GRAD_Q, plane, lambda p: grad_mine.at[p], grad_q)
    sent_all(GRAD_N, near, lambda p: grad_n.at[z], grad_n)
    wait_all(QMF_X, row_x, qmf_x)
    qm_force_ref[...] = total(qmf_x, nx) * (grad_sum[pl.ds(z, 1), :] * coupling)
    sent_all(QMF_X, row_x, lambda p: qmf_x.at[x], qmf_x)
    sent_all(MMF_Q, plane, lambda p: mmf_mine.at[p], mmf_q)
    wait_all(MMF_Q, plane, mmf_q)
    mm_force_ref[...] = total(mmf_q, nq) * (charge_ref[...] * -coupling)


def on_device(
    nz,
    nq,
    nr,
    qm_pos,
    species,
    qm_count,
    ghost_owner,
    ghost_slot,
    mm_pos,
    mm_charge,
    species_table,
    potential_gain,
    message_weight,
    hidden_weight,
    energy_readout,
    charge_readout,
):
    atoms = qm_pos.shape[1]
    mm_here = mm_pos.shape[1]
    nx = nr // 2
    coupling = float(mm_here * nz * nq * nr) ** (-0.5)
    here = nz * atoms
    groups = ghost_owner.shape[1] + 1
    hot_rows = -(-nz * nq // 16) * 16
    small = lambda *shape: pltpu.VMEM(shape, F32)
    vmem = pl.BlockSpec(memory_space=pltpu.VMEM)
    atom_energy, qm_force, mm_force = pl.pallas_call(
        functools.partial(kernel, nz, nq, nx, coupling),
        out_shape=(
            jax.ShapeDtypeStruct((1, atoms), F32),
            jax.ShapeDtypeStruct((3, atoms), F32),
            jax.ShapeDtypeStruct((3, mm_here), F32),
        ),
        in_specs=[vmem] * 13,
        out_specs=(vmem,) * 3,
        scratch_shapes=[
            small(nq, 4, mm_here),
            small(nz, 4, atoms),
            small(nx, nz, atoms),
            small(2 * nz, nz, atoms),
            small(nq, 2 * nz, atoms),
            small(nq, nz, atoms),
            small(nq, nz, atoms),
            small(nz, nz, atoms),
            small(nz, atoms),
            small(nz, 3, atoms),
            small(2 * nz, 3, atoms),
            small(nx, 3, atoms),
            small(nq, 3, mm_here),
            small(nq, 3, mm_here),
            *[small(here, LANES)] * 10,
            small(nq, here, mm_here),
            small(LANES, LANES),
            pltpu.VMEM((groups * atoms, LANES), BF16),
            pltpu.VMEM((hot_rows, groups * atoms), BF16),
            small(groups * atoms, LANES),
            pltpu.SemaphoreType.DMA((10, max(2 * nz, nq, nx))),
            pltpu.SemaphoreType.DMA((10, max(2 * nz, nq, nx))),
        ],
        compiler_params=pltpu.CompilerParams(
            collective_id=0, has_side_effects=True, vmem_limit_bytes=48 * 2**20
        ),
    )(
        qm_pos,
        species[None, :],
        qm_count[None, :],
        ghost_owner,
        ghost_slot,
        mm_pos,
        mm_charge[None, :],
        species_table,
        potential_gain[None, :],
        message_weight,
        hidden_weight,
        energy_readout[None, :],
        charge_readout[None, :],
    )
    return (atom_energy[0], qm_force, mm_force)


def solution(mesh):
    blocks, nr = mesh.shape["blk"], mesh.shape["rep"]
    nq = min(8, blocks // 2)
    placed = (
        P(None, "blk"),
        P("blk"),
        P("blk"),
        P("blk", None),
        P("blk", None),
        P(None, ("blk", "rep")),
        P(("blk", "rep")),
        P(),
        P(),
        P(),
        P(),
        P(),
        P(),
    )
    return jax.shard_map(
        functools.partial(on_device, blocks // nq, nq, nr),
        mesh=mesh,
        in_specs=placed,
        out_specs=(P("blk"), P(None, "blk"), P(None, ("blk", "rep"))),
        check_vma=False,
    )
```

time: 101 us -> 73.4 us (0.73)
  Pallas kernels: 95.4 us -> 68 us
    pallas_call x1, Pallas kernels: 95.4 us -> 68 us  [on_device(): pl.pallas_call(functools.partial(kernel, nz, nq, nx, coupling), out_shape...]
where the time goes in v2:
time: 73.4 us; the launch traced here: 73.2 us
  Pallas kernels  68 us (93%)
  local copies, waits for them, and re-layouts  3.78 us (5%)
  between operations  1.38 us (2%)
    pallas_call x1, Pallas kernels, on_device(): pl.pallas_call(functools.partial(kernel, nz, nq, nx, coupling), out_shape...  68 us
    unnamed x29, local copies, waits for them, and re-layouts  3.78 us

profile of v2, /device:TPU:1, one launch (start us, length us, event | category | flops | bytes accessed | tf_op | source)
XLA Modules:
  0.0 73.2 jit_solution(7253598664389400600)
XLA Ops:
  1.3 0.0 copy-start.10
  1.3 0.7 copy-done.10
  2.0 0.0 copy-start.11
  2.0 0.0 copy-start
  2.0 0.1 copy.16.owner_ref
  2.1 0.6 copy-done.11
  2.6 0.0 copy-start.1
  2.6 0.0 copy-start.2
  2.6 0.0 copy-start.3
  2.6 0.0 copy-start.4
  2.7 0.0 copy-start.5
  2.7 0.0 copy-start.6
  2.7 0.0 copy-start.7
  2.7 0.0 copy-start.8
  2.7 0.0 copy-start.9
  2.7 0.1 copy.17.slot_ref
  2.8 0.0 copy-done
  2.8 0.6 copy-done.1
  3.4 0.0 copy-done.2
  3.4 0.0 copy-done.3
  3.4 0.0 copy-done.4
  3.4 0.0 copy-done.5
  3.4 0.0 copy-done.6
  3.4 0.0 copy-done.7
  3.4 0.0 copy-done.8
  3.5 0.0 copy-done.9
  3.5 68.0 %shard_map.148 = (f32[1,128]{1,0:T(1,128)S(1)}, f32[3,128]{1,0:T(4,128)S(1)}, f32[3,512]{1,0:T(4,128)S(1)}) custom-call(f32[3,128]{1,0:T(4,128)S(1)} %copy-done.3, s32[1,128]{1,0:T(1,128)S(1)} %bitcast.11, s32[1,1]{1,0:T(1,128)} %bitcast.7.count_ref, s32[128,4]{1,0:T(8,128)S(1)} %copy.16.owner_ref, s32[128,4]{1,0:T(8,128)S(1)} %copy.17.slot_ref, ...), custom_call_target="tpu_custom_call" | custom-call | tf_op jit(solution)/shard_map/pallas_call | solution.py:446
  71.5 0.5 copy.22
  72.0 0.6 copy.23
  72.6 0.6 copy.24
Async XLA Ops:
  1.3 0.7 copy-start.10
  2.0 0.7 copy-start.11
  2.0 0.9 %copy-start = (bf16[128,256]{1,0:T(8,128)(2,1)S(1)}, bf16[128,256]{1,0:T(8,128)(2,1)}, u32[]{:S(2)}) copy-start(bf16[128,256]{1,0:T(8,128)(2,1)} %hidden_ref.1) | copy-start | bytes 196612
  2.6 0.8 %copy-start.1 = (bf16[128,128]{1,0:T(8,128)(2,1)S(1)}, bf16[128,128]{1,0:T(8,128)(2,1)}, u32[]{:S(2)}) copy-start(bf16[128,128]{1,0:T(8,128)(2,1)} %message_ref.1) | copy-start | bytes 98308
  2.6 0.8 %copy-start.2 = (f32[3,512]{1,0:T(4,128)S(1)}, f32[3,512]{1,0:T(4,128)}, u32[]{:S(2)}) copy-start(f32[3,512]{1,0:T(4,128)} %mm_ref.1) | copy-start | bytes 18436
  2.6 0.8 %copy-start.3 = (f32[3,128]{1,0:T(4,128)S(1)}, f32[3,128]{1,0:T(4,128)}, u32[]{:S(2)}) copy-start(f32[3,128]{1,0:T(4,128)} %qm_ref.1) | copy-start | bytes 4612
  2.6 0.8 %copy-start.4 = (f32[512]{0:T(512)S(1)}, f32[512]{0:T(512)}, u32[]{:S(2)}) copy-start(f32[512]{0:T(512)} %param.19) | copy-start | bytes 6148
  2.7 0.8 %copy-start.5 = (bf16[8,128]{1,0:T(8,128)(2,1)S(1)}, bf16[8,128]{1,0:T(8,128)(2,1)}, u32[]{:S(2)}) copy-start(bf16[8,128]{1,0:T(8,128)(2,1)} %table_ref.1) | copy-start | bytes 6148
  2.7 0.8 %copy-start.6 = (f32[256]{0:T(256)S(1)}, f32[256]{0:T(256)}, u32[]{:S(2)}) copy-start(f32[256]{0:T(256)} %param.24) | copy-start | bytes 3076
  2.7 0.8 %copy-start.7 = (f32[256]{0:T(256)S(1)}, f32[256]{0:T(256)}, u32[]{:S(2)}) copy-start(f32[256]{0:T(256)} %param.25) | copy-start | bytes 3076
  2.7 0.8 %copy-start.8 = (s32[128]{0:T(128)S(1)}, s32[128]{0:T(128)}, u32[]{:S(2)}) copy-start(s32[128]{0:T(128)} %param.14) | copy-start | bytes 1540
  2.7 0.8 %copy-start.9 = (f32[128]{0:T(128)S(1)}, f32[128]{0:T(128)}, u32[]{:S(2)}) copy-start(f32[128]{0:T(128)} %param.21) | copy-start | bytes 1540

commit v3 on v2

--- a/solution.py
+++ b/solution.py
@@ -9,7 +9,6 @@
 
 SOFTEN = 0.25
 LANES = 128
-POT_ROWS = 64
 FORCE_ROWS = 32
 EARLY = 2
 MESH = pl.DeviceIdType.MESH
@@ -65,14 +64,14 @@
     wide_x,
     wide_y,
     wide_z,
-    wide_e,
-    wide_ex,
-    wide_ey,
-    wide_ez,
     acc_x,
     acc_y,
     acc_z,
     inverses,
+    qm_parts,
+    mm_parts,
+    charges,
+    qm_lines,
     table_wide,
     owner_hot,
     owner_hot_t,
@@ -88,7 +87,7 @@
     atoms = qm_ref.shape[1]
     mm_tiles = mm_ref.shape[1] // LANES
     blocks = nz * nq
-    neighbours = owner_ref.shape[1]
+    neighbours = owner_ref.shape[0]
 
     def at_ring(p):
         return ((p % nz) * nq + q, x * 2 + p // nz)
@@ -97,7 +96,7 @@
         return (z * nq + p, rep)
 
     def shift(d):
-        return jnp.where(d < nz // 2, d, d - nz)
+        return (d + 1) // 2 * (2 * (d % 2) - 1)
 
     def q_place(d, sign):
         y = (q // 2 + (nq // 2) + sign * (d // 2)) % (nq // 2)
@@ -181,16 +180,15 @@
     for k in range(neighbours + 1):
         rows = slice(k * atoms, (k + 1) * atoms)
         if k < neighbours:
-            owner = owner_ref[:, k : k + 1]
-            hot = (lane == (owner % nq) * nz + owner // nq).astype(F32)
-            slots = (lane == slot_ref[:, k : k + 1]).astype(F32)
+            owner = owner_ref[k : k + 1, :]
+            hot_t = (row == (owner % nq) * nz + owner // nq).astype(F32)
+            slots = jnp.transpose((row == slot_ref[k : k + 1, :]).astype(F32))
         else:
-            hot = (lane == q * nz + z).astype(F32)
+            hot_t = (row == q * nz + z).astype(F32)
             slots = (lane == row).astype(F32)
-        owner_hot[rows, :] = hot.astype(BF16)
-        owner_hot_t[:, rows] = jnp.transpose(hot)[0 : owner_hot_t.shape[0], :].astype(BF16)
+        owner_hot[rows, :] = jnp.transpose(hot_t).astype(BF16)
+        owner_hot_t[:, rows] = hot_t[0 : owner_hot_t.shape[0], :].astype(BF16)
         slot_hot[rows, :] = slots
-    acc_x[...] = jnp.zeros_like(acc_x)
 
     def wide(line):
         return jnp.transpose(jnp.broadcast_to(line, (LANES, atoms)))
@@ -198,15 +196,59 @@
     def block_rows(p):
         return pl.ds(pl.multiple_of(p * atoms, atoms), atoms)
 
-    def widen(p):
+    def widen(p, carry):
         rows = block_rows(p)
         wide_x[rows, :] = wide(qm_all[p, 0:1, :])
         wide_y[rows, :] = wide(qm_all[p, 1:2, :])
         wide_z[rows, :] = wide(qm_all[p, 2:3, :])
         pot_q[q, pl.ds(nz + p, 1), :] = qm_all[p, 3:4, :]
-
-    widen(z)
-    each(near, lambda d: widen(wait_from(QM_N, near, d, qm_all)))
+        return carry
+
+    def chunk_columns(p):
+        return pl.ds(pl.multiple_of(p * mm_tiles * LANES, LANES), mm_tiles * LANES)
+
+    def stacked(place, norm_first, order):
+        norm = jnp.sum(place * place, axis=0, keepdims=True)
+        one, nothing = jnp.ones_like(norm), jnp.zeros((3, norm.shape[1]), F32)
+        if norm_first:
+            record = jnp.concatenate([place, norm, one, nothing], axis=0)
+        else:
+            record = jnp.concatenate([-2.0 * place, one, norm + SOFTEN, nothing], axis=0)
+        pieces = [piece.astype(F32) for piece in split3(record)]
+        return jnp.concatenate([pieces[k] for k in order], axis=0)
+
+    def take_charges(p):
+        where = chunk_columns(p)
+        mm_parts[:, where] = stacked(mm_all[p, 0:3, :], True, (0, 1, 0, 1, 2, 0)).astype(BF16)
+        charges[:, where] = mm_all[p, 3:4, :]
+
+    take_charges(q)
+    each(plane, lambda d: take_charges(wait_from(MM_Q, plane, d, mm_all)))
+
+    def potential_block(d):
+        p = jnp.where(d > 0, near[5](near[3](d)), z)
+        rows = block_rows(p)
+        parts = stacked(qm_all[p, 0:3, :], False, (0, 0, 1, 1, 0, 2))
+        parts = jnp.concatenate([parts, jnp.zeros((LANES - 48, atoms), F32)], axis=0)
+        parts = jnp.transpose(parts).astype(BF16)
+        square = jnp.dot(parts[:, 0:48], mm_parts[...], preferred_element_type=F32)
+        inverse = lax.rsqrt(square)
+        inverses[rows, :] = inverse
+        term = inverse * charges[...]
+        running = term[:, 0:LANES]
+        for t in range(1, nq * mm_tiles):
+            running = running + term[:, t * LANES : (t + 1) * LANES]
+        pot_x[x, pl.ds(p, 1), :] = jnp.sum(jnp.transpose(running), axis=0, keepdims=True)
+
+    def potential_step(d, carry):
+        @pl.when(d > 0)
+        def _():
+            wait_from(QM_N, near, d, qm_all)
+
+        potential_block(d)
+        return carry
+
+    lax.fori_loop(0, nz, potential_step, 0)
 
     def columns(chunk):
         return [
@@ -214,42 +256,18 @@
             for t in range(mm_tiles)
         ]
 
-    def potential_chunk(d, carry):
-        @pl.when(d > 0)
-        def _():
-            wait_from(MM_Q, plane, d, mm_all)
-
-        chunk = plane[3](d)
-        tiles = columns(chunk)
-
-        def group(g, inner):
-            rows = pl.ds(pl.multiple_of(g * POT_ROWS, POT_ROWS), POT_ROWS)
-            px, py, pz = wide_x[rows, :], wide_y[rows, :], wide_z[rows, :]
-            running = acc_x[rows, :]
-            for t, (mx, my, mz, mq) in enumerate(tiles):
-                dx, dy, dz = px - mx, py - my, pz - mz
-                inverse = lax.rsqrt(dx * dx + dy * dy + (dz * dz + SOFTEN))
-                inverses[chunk, rows, t * LANES : (t + 1) * LANES] = inverse
-                running = running + inverse * mq
-            acc_x[rows, :] = running
-            return inner
-
-        return lax.fori_loop(0, nz * atoms // POT_ROWS, group, carry)
-
-    lax.fori_loop(0, nq, potential_chunk, 0)
-
     def lines(acc, p):
         return jnp.sum(jnp.transpose(acc[block_rows(p), :]), axis=0, keepdims=True)
 
-    def gather_potential(p, carry):
-        pot_x[x, pl.ds(p, 1), :] = lines(acc_x, p)
-        return carry
-
-    lax.fori_loop(0, nz, gather_potential, 0)
     send_all(POT_X, row_x, lambda p: pot_x.at[x], pot_x)
     acc_x[...] = jnp.zeros_like(acc_x)
     acc_y[...] = jnp.zeros_like(acc_y)
     acc_z[...] = jnp.zeros_like(acc_z)
+    lax.fori_loop(0, nz, widen, 0)
+    qm_lines[0:1, :] = jnp.ones((1, nz * atoms), F32)
+    for p in range(nz):
+        qm_lines[1:4, p * atoms : (p + 1) * atoms] = qm_all[p, 0:3, :]
+    qm_lines[4:8, :] = jnp.zeros((4, nz * atoms), F32)
 
     def pull_chunk(chunk, carry):
         tiles = columns(chunk)
@@ -259,10 +277,10 @@
             px, py, pz = wide_x[rows, :], wide_y[rows, :], wide_z[rows, :]
             fx, fy, fz = acc_x[rows, :], acc_y[rows, :], acc_z[rows, :]
             for t, (mx, my, mz, mq) in enumerate(tiles):
-                where = slice(t * LANES, (t + 1) * LANES)
-                inverse = inverses[chunk, rows, where]
+                where = pl.ds(pl.multiple_of((chunk * mm_tiles + t) * LANES, LANES), LANES)
+                inverse = inverses[rows, where]
                 cube = inverse * inverse * inverse
-                inverses[chunk, rows, where] = cube
+                inverses[rows, where] = cube
                 pull = cube * mq
                 fx = fx + pull * (px - mx)
                 fy = fy + pull * (py - my)
@@ -358,39 +376,22 @@
     live_plane = (pot_q[q, nz : 2 * nz, :] >= 0).astype(F32)
     grad_sum[...] = live_plane * total(grad_n, nz)
 
-    def widen_effective(p, carry):
-        rows = block_rows(p)
-        effective = wide(grad_sum[pl.ds(p, 1), :])
-        wide_e[rows, :] = effective
-        wide_ex[rows, :] = effective * wide_x[rows, :]
-        wide_ey[rows, :] = effective * wide_y[rows, :]
-        wide_ez[rows, :] = effective * wide_z[rows, :]
-        return carry
-
-    lax.fori_loop(0, nz, widen_effective, 0)
+    effective = jnp.concatenate([grad_sum[p : p + 1, :] for p in range(nz)], axis=1)
+    weights = qm_lines[...] * effective
+    high = weights.astype(BF16).astype(F32)
+    weights = jnp.concatenate([high, weights - high], axis=0).astype(BF16)
 
     def push_chunk(step, carry):
         d = nq - step
         chunk = jnp.where(d > 0, plane[2](d), q)
 
-        def group(g, running):
-            rows = pl.ds(pl.multiple_of(g * FORCE_ROWS, FORCE_ROWS), FORCE_ROWS)
-            weights = wide_e[rows, :], wide_ex[rows, :], wide_ey[rows, :], wide_ez[rows, :]
-            after = []
-            for t in range(mm_tiles):
-                cube = inverses[chunk, rows, t * LANES : (t + 1) * LANES]
-                for c, weight in enumerate(weights):
-                    term = jnp.sum((cube * weight).reshape(FORCE_ROWS // 8, 8, LANES), axis=0)
-                    after.append(running[4 * t + c] + term)
-            return tuple(after)
-
-        nothing = tuple(jnp.zeros((8, LANES), F32) for _ in range(4 * mm_tiles))
-        sums = lax.fori_loop(0, nz * atoms // FORCE_ROWS, group, nothing)
-        for t in range(mm_tiles):
-            where = slice(t * LANES, (t + 1) * LANES)
-            plain, *moments = [jnp.sum(sums[4 * t + c], axis=0, keepdims=True) for c in range(4)]
-            for c in range(3):
-                mmf_mine[chunk, c : c + 1, where] = moments[c] - plain * mm_all[chunk, c : c + 1, where]
+        cube = inverses[:, chunk_columns(chunk)]
+        high = cube.astype(BF16)
+        low = (cube - high.astype(F32)).astype(BF16)
+        sums = jnp.dot(weights, high, preferred_element_type=F32)
+        sums = sums + jnp.dot(weights, low, preferred_element_type=F32)
+        sums = sums[0:8, :] + sums[8:16, :]
+        mmf_mine[chunk] = sums[1:4, :] - sums[0:1, :] * mm_all[chunk, 0:3, :]
 
         @pl.when(d > 0)
         def _():
@@ -467,8 +468,12 @@
             small(nx, 3, atoms),
             small(nq, 3, mm_here),
             small(nq, 3, mm_here),
-            *[small(here, LANES)] * 10,
-            small(nq, here, mm_here),
+            *[small(here, LANES)] * 6,
+            small(here, nq * mm_here),
+            pltpu.VMEM((here, LANES), BF16),
+            pltpu.VMEM((48, nq * mm_here), BF16),
+            small(1, nq * mm_here),
+            small(8, here),
             small(LANES, LANES),
             pltpu.VMEM((groups * atoms, LANES), BF16),
             pltpu.VMEM((hot_rows, groups * atoms), BF16),
@@ -483,8 +488,8 @@
         qm_pos,
         species[None, :],
         qm_count[None, :],
-        ghost_owner,
-        ghost_slot,
+        ghost_owner.T,
+        ghost_slot.T,
         mm_pos,
         mm_charge[None, :],
         species_table,

time: 73.4 us -> 68.2 us (0.929)
  Pallas kernels: 68 us -> 59.8 us
  local copies, waits for them, and re-layouts: 3.78 us -> 6.65 us
    pallas_call x1, Pallas kernels: 68 us -> 59.8 us  [on_device(): pl.pallas_call(functools.partial(kernel, nz, nq, nx, coupling), out_shape...]
    unnamed x29 -> x27, local copies, waits for them, and re-layouts: 3.78 us -> 6.65 us
where the time goes in v3:
time: 68.2 us; the launch traced here: 67.9 us
  Pallas kernels  59.8 us (88%)
  local copies, waits for them, and re-layouts  6.65 us (10%)
  between operations  1.37 us (2%)
    pallas_call x1, Pallas kernels, on_device(): pl.pallas_call(functools.partial(kernel, nz, nq, nx, coupling), out_shape...  59.8 us
    unnamed x27, local copies, waits for them, and re-layouts  6.65 us

profile of v3, /device:TPU:1, one launch (start us, length us, event | category | flops | bytes accessed | tf_op | source)
XLA Modules:
  0.0 67.9 jit_solution(293689501766893933)
XLA Ops:
  0.6 0.0 copy-start.6
  1.3 0.0 copy-start.2
  1.3 0.0 copy-start.5
  1.3 0.0 copy-start.4
  1.3 0.0 copy-start.3
  1.3 0.0 copy-start.8
  1.4 0.0 copy-done.6
  1.4 0.6 copy-done.2
  2.0 0.0 copy-done.5
  2.0 0.0 copy-done.4
  2.0 0.0 copy-done.3
  2.0 0.0 copy-done.8
  2.0 0.0 copy-start
  2.0 0.8 %copy-done = bf16[128,256]{1,0:T(8,128)(2,1)S(1)} copy-done((bf16[128,256]{1,0:T(8,128)(2,1)S(1)}, bf16[128,256]{1,0:T(8,128)(2,1)}, u32[]{:S(2)}) %copy-start) | copy-done | bytes 65560
  2.9 0.0 copy-start.1
  2.9 0.8 %copy-done.1 = bf16[128,128]{1,0:T(8,128)(2,1)S(1)} copy-done((bf16[128,128]{1,0:T(8,128)(2,1)S(1)}, bf16[128,128]{1,0:T(8,128)(2,1)}, u32[]{:S(2)}) %copy-start.1) | copy-done | bytes 32792
  3.6 0.0 copy-start.7
  3.6 0.7 %copy-done.7 = bf16[8,128]{1,0:T(8,128)(2,1)S(1)} copy-done((bf16[8,128]{1,0:T(8,128)(2,1)S(1)}, bf16[8,128]{1,0:T(8,128)(2,1)}, u32[]{:S(2)}) %copy-start.7) | copy-done | bytes 2072
  4.3 0.0 copy-start.9
  4.3 0.7 copy-done.9
  5.0 0.0 copy-start.10
  5.0 0.7 copy-done.10
  5.7 0.0 copy-start.11
  5.7 0.7 copy-done.11
  6.3 59.8 %shard_map.148 = (f32[1,128]{1,0:T(1,128)S(1)}, f32[3,128]{1,0:T(4,128)S(1)}, f32[3,512]{1,0:T(4,128)S(1)}) custom-call(f32[3,128]{1,0:T(4,128)S(1)} %copy-done.3, s32[1,128]{1,0:T(1,128)S(1)} %bitcast.15, s32[1,1]{1,0:T(1,128)} %bitcast.9.count_ref, s32[4,128]{1,0:T(4,128)S(1)} %bitcast.10, s32[4,128]{1,0:T(4,128)S(1)} %bitcast.11, f32[3,512]{1,0:T(4,128)S(1)} %copy-done.2, ...), custom_call_target="tpu_custom_call" | custom-call | tf_op jit(solution)/shard_map/pallas_call | solution.py:447
  66.2 0.5 copy.20
  66.7 0.6 copy.21
  67.3 0.6 copy.22
Async XLA Ops:
  0.6 0.7 %copy-start.6 = (f32[512]{0:T(512)S(1)}, f32[512]{0:T(512)}, u32[]{:S(2)}) copy-start(f32[512]{0:T(512)} %param.19) | copy-start | bytes 6148
  1.3 0.7 %copy-start.2 = (f32[3,512]{1,0:T(4,128)S(1)}, f32[3,512]{1,0:T(4,128)}, u32[]{:S(2)}) copy-start(f32[3,512]{1,0:T(4,128)} %mm_ref.1) | copy-start | bytes 18436
  1.3 0.7 %copy-start.5 = (s32[128,4]{0,1:T(4,128)S(1)}, s32[128,4]{0,1:T(4,128)}, u32[]{:S(2)}) copy-start(s32[128,4]{0,1:T(4,128)} %param.17) | copy-start | bytes 6148
  1.3 0.7 %copy-start.4 = (s32[128,4]{0,1:T(4,128)S(1)}, s32[128,4]{0,1:T(4,128)}, u32[]{:S(2)}) copy-start(s32[128,4]{0,1:T(4,128)} %param.16) | copy-start | bytes 6148
  1.3 0.7 %copy-start.3 = (f32[3,128]{1,0:T(4,128)S(1)}, f32[3,128]{1,0:T(4,128)}, u32[]{:S(2)}) copy-start(f32[3,128]{1,0:T(4,128)} %qm_ref.1) | copy-start | bytes 4612
  1.3 0.7 %copy-start.8 = (f32[256]{0:T(256)S(1)}, f32[256]{0:T(256)}, u32[]{:S(2)}) copy-start(f32[256]{0:T(256)} %param.24) | copy-start | bytes 3076
  2.0 0.8 %copy-start = (bf16[128,256]{1,0:T(8,128)(2,1)S(1)}, bf16[128,256]{1,0:T(8,128)(2,1)}, u32[]{:S(2)}) copy-start(bf16[128,256]{1,0:T(8,128)(2,1)} %hidden_ref.1) | copy-start | bytes 196612
  2.9 0.8 %copy-start.1 = (bf16[128,128]{1,0:T(8,128)(2,1)S(1)}, bf16[128,128]{1,0:T(8,128)(2,1)}, u32[]{:S(2)}) copy-start(bf16[128,128]{1,0:T(8,128)(2,1)} %message_ref.1) | copy-start | bytes 98308
  3.6 0.7 %copy-start.7 = (bf16[8,128]{1,0:T(8,128)(2,1)S(1)}, bf16[8,128]{1,0:T(8,128)(2,1)}, u32[]{:S(2)}) copy-start(bf16[8,128]{1,0:T(8,128)(2,1)} %table_ref.1) | copy-start | bytes 6148
  4.3 0.7 %copy-start.9 = (f32[256]{0:T(256)S(1)}, f32[256]{0:T(256)}, u32[]{:S(2)}) copy-start(f32[256]{0:T(256)} %param.25) | copy-start | bytes 3076
  5.0 0.7 copy-start.10
  5.7 0.7 copy-start.11

commit v4 on v3

--- a/solution.py
+++ b/solution.py
@@ -11,6 +11,7 @@
 LANES = 128
 FORCE_ROWS = 32
 EARLY = 2
+TABLE = 7
 MESH = pl.DeviceIdType.MESH
 F32 = jnp.float32
 BF16 = jnp.bfloat16
@@ -31,19 +32,19 @@
     nq,
     nx,
     coupling,
-    qm_ref,
-    species_ref,
-    count_ref,
-    owner_ref,
-    slot_ref,
-    mm_ref,
-    charge_ref,
+    qm_hbm,
+    species_hbm,
+    count_hbm,
+    owner_hbm,
+    slot_hbm,
+    mm_hbm,
+    charge_hbm,
     table_ref,
-    gain_ref,
-    message_ref,
-    hidden_ref,
-    energy_ref,
-    readout_ref,
+    gain_hbm,
+    message_hbm,
+    hidden_hbm,
+    energy_hbm,
+    readout_hbm,
     atom_energy_ref,
     qm_force_ref,
     mm_force_ref,
@@ -68,7 +69,6 @@
     acc_y,
     acc_z,
     inverses,
-    qm_parts,
     mm_parts,
     charges,
     qm_lines,
@@ -76,6 +76,19 @@
     owner_hot,
     owner_hot_t,
     slot_hot,
+    qm_ref,
+    species_ref,
+    count_ref,
+    owner_ref,
+    slot_ref,
+    mm_ref,
+    charge_ref,
+    gain_ref,
+    message_ref,
+    hidden_ref,
+    energy_ref,
+    readout_ref,
+    fetch_sems,
     send_sems,
     recv_sems,
 ):
@@ -155,13 +168,42 @@
             result = result + buffer[p]
         return result
 
+    fetches = [
+        pltpu.make_async_copy(src, dst, fetch_sems.at[k])
+        for k, (src, dst) in enumerate(
+            [
+                (mm_hbm, mm_ref),
+                (charge_hbm, charge_ref),
+                (qm_hbm, qm_ref),
+                (species_hbm, species_ref),
+                (count_hbm, count_ref),
+                (owner_hbm, owner_ref),
+                (slot_hbm, slot_ref),
+                (gain_hbm, gain_ref),
+                (message_hbm, message_ref),
+                (hidden_hbm, hidden_ref),
+                (energy_hbm, energy_ref),
+                (readout_hbm, readout_ref),
+            ]
+        )
+    ]
+    for fetch in fetches:
+        fetch.start()
+
     barrier = pltpu.get_barrier_semaphore()
-    for axis in (far, plane, row_x):
-
-        def greet(d, axis=axis):
-            pl.semaphore_signal(barrier, inc=1, device_id=axis[4](axis[2](d)), device_id_type=MESH)
-
-        each(axis, greet)
+    def greet(device):
+        pl.semaphore_signal(barrier, inc=1, device_id=device, device_id_type=MESH)
+
+    def greet_ring(d, carry):
+        greet(at_ring((ring + d) % rings))
+        greet(at_ring((ring + rings - d) % rings))
+        return carry
+
+    lax.fori_loop(1, nz // 2 + 1, greet_ring, 0)
+    each(plane, lambda d: greet(at_q(plane[2](d))))
+    each(row_x, lambda d: greet(row_x[4](row_x[2](d))))
+    for fetch in fetches[:5]:
+        fetch.wait()
 
     mm_all[q, 0:3, :] = mm_ref[...]
     mm_all[q, 3:4, :] = charge_ref[...]
@@ -169,10 +211,12 @@
     qm_all[z, 0:3, :] = qm_ref[...]
     qm_all[z, 3:4, :] = jnp.where(live_row, species_ref[...], -1).astype(F32)
 
-    pl.semaphore_wait(barrier, rings + nq + nx - 3)
+    pl.semaphore_wait(barrier, nz + nq + nx - 2)
     send_all(QM_N, near, lambda p: qm_all.at[z], qm_all)
     send_all(MM_Q, plane, lambda p: mm_all.at[q], mm_all)
 
+    for fetch in fetches[5:]:
+        fetch.wait()
     table_wide[...] = jnp.zeros_like(table_wide)
     table_wide[0 : table_ref.shape[0], :] = table_ref[...].astype(F32)
     lane = lax.broadcasted_iota(jnp.int32, (atoms, LANES), 1)
@@ -225,30 +269,32 @@
     take_charges(q)
     each(plane, lambda d: take_charges(wait_from(MM_Q, plane, d, mm_all)))
 
-    def potential_block(d):
-        p = jnp.where(d > 0, near[5](near[3](d)), z)
-        rows = block_rows(p)
+    def take_block(p):
         parts = stacked(qm_all[p, 0:3, :], False, (0, 0, 1, 1, 0, 2))
         parts = jnp.concatenate([parts, jnp.zeros((LANES - 48, atoms), F32)], axis=0)
-        parts = jnp.transpose(parts).astype(BF16)
-        square = jnp.dot(parts[:, 0:48], mm_parts[...], preferred_element_type=F32)
+        return jnp.transpose(parts).astype(BF16)[:, 0:48]
+
+    def potential_step(k, carry):
+        @pl.when(k > 0)
+        def _():
+            wait_from(QM_N, near, 2 * k, qm_all)
+
+        wait_from(QM_N, near, 2 * k + 1, qm_all)
+        pair = [jnp.where(k > 0, near[5](near[3](2 * k)), z), near[5](near[3](2 * k + 1))]
+        parts = jnp.concatenate([take_block(p) for p in pair], axis=0)
+        square = jnp.dot(parts, mm_parts[...], preferred_element_type=F32)
         inverse = lax.rsqrt(square)
-        inverses[rows, :] = inverse
         term = inverse * charges[...]
         running = term[:, 0:LANES]
         for t in range(1, nq * mm_tiles):
             running = running + term[:, t * LANES : (t + 1) * LANES]
-        pot_x[x, pl.ds(p, 1), :] = jnp.sum(jnp.transpose(running), axis=0, keepdims=True)
-
-    def potential_step(d, carry):
-        @pl.when(d > 0)
-        def _():
-            wait_from(QM_N, near, d, qm_all)
-
-        potential_block(d)
+        for k, p in enumerate(pair):
+            rows = slice(k * atoms, (k + 1) * atoms)
+            inverses[block_rows(p), :] = inverse[rows, :]
+            pot_x[x, pl.ds(p, 1), :] = jnp.sum(jnp.transpose(running[rows, :]), axis=0, keepdims=True)
         return carry
 
-    lax.fori_loop(0, nz, potential_step, 0)
+    lax.fori_loop(0, nz // 2, potential_step, 0)
 
     def columns(chunk):
         return [
@@ -297,6 +343,9 @@
     send_all(POT_Z, far, lambda p: pot_z.at[ring], pot_z)
     lax.fori_loop(early, nq, pull_chunk, 0)
 
+    wait_all(POT_Z, far, pot_z)
+    pot_q[q, 0:nz, :] = total(pot_z, rings) * coupling
+    send_all(POT_Q, plane, lambda p: pot_q.at[q], pot_q)
     def gather_force(p, carry):
         qmf_mine[p, 0:1, :] = lines(acc_x, p)
         qmf_mine[p, 1:2, :] = lines(acc_y, p)
@@ -305,9 +354,6 @@
 
     lax.fori_loop(0, nz, gather_force, 0)
     qmf_z[ring] = qmf_mine[z]
-    wait_all(POT_Z, far, pot_z)
-    pot_q[q, 0:nz, :] = total(pot_z, rings) * coupling
-    send_all(POT_Q, plane, lambda p: pot_q.at[q], pot_q)
     send_all(QMF_Z, far, lambda p: qmf_mine.at[p % nz], qmf_z)
     wait_all(POT_Q, plane, pot_q)
 
@@ -442,8 +488,24 @@
     here = nz * atoms
     groups = ghost_owner.shape[1] + 1
     hot_rows = -(-nz * nq // 16) * 16
+    arguments = (
+        qm_pos,
+        species[None, :],
+        qm_count[None, :],
+        ghost_owner.T,
+        ghost_slot.T,
+        mm_pos,
+        mm_charge[None, :],
+        species_table,
+        potential_gain[None, :],
+        message_weight,
+        hidden_weight,
+        energy_readout[None, :],
+        charge_readout[None, :],
+    )
     small = lambda *shape: pltpu.VMEM(shape, F32)
     vmem = pl.BlockSpec(memory_space=pltpu.VMEM)
+    hbm = pl.BlockSpec(memory_space=pltpu.HBM)
     atom_energy, qm_force, mm_force = pl.pallas_call(
         functools.partial(kernel, nz, nq, nx, coupling),
         out_shape=(
@@ -451,7 +513,7 @@
             jax.ShapeDtypeStruct((3, atoms), F32),
             jax.ShapeDtypeStruct((3, mm_here), F32),
         ),
-        in_specs=[vmem] * 13,
+        in_specs=[hbm] * 7 + [vmem] + [hbm] * 5,
         out_specs=(vmem,) * 3,
         scratch_shapes=[
             small(nq, 4, mm_here),
@@ -470,7 +532,6 @@
             small(nq, 3, mm_here),
             *[small(here, LANES)] * 6,
             small(here, nq * mm_here),
-            pltpu.VMEM((here, LANES), BF16),
             pltpu.VMEM((48, nq * mm_here), BF16),
             small(1, nq * mm_here),
             small(8, here),
@@ -478,27 +539,15 @@
             pltpu.VMEM((groups * atoms, LANES), BF16),
             pltpu.VMEM((hot_rows, groups * atoms), BF16),
             small(groups * atoms, LANES),
+            *[pltpu.VMEM(a.shape, a.dtype) for k, a in enumerate(arguments) if k != TABLE],
+            pltpu.SemaphoreType.DMA((12,)),
             pltpu.SemaphoreType.DMA((10, max(2 * nz, nq, nx))),
             pltpu.SemaphoreType.DMA((10, max(2 * nz, nq, nx))),
         ],
         compiler_params=pltpu.CompilerParams(
-            collective_id=0, has_side_effects=True, vmem_limit_bytes=48 * 2**20
+            collective_id=0, has_side_effects=True, vmem_limit_bytes=56 * 2**20
         ),
-    )(
-        qm_pos,
-        species[None, :],
-        qm_count[None, :],
-        ghost_owner.T,
-        ghost_slot.T,
-        mm_pos,
-        mm_charge[None, :],
-        species_table,
-        potential_gain[None, :],
-        message_weight,
-        hidden_weight,
-        energy_readout[None, :],
-        charge_readout[None, :],
-    )
+    )(*arguments)
     return (atom_energy[0], qm_force, mm_force)
 
 

time: 68.2 us -> 62.6 us (0.918)
  local copies, waits for them, and re-layouts: 6.65 us -> 3 us
  Pallas kernels: 59.8 us -> 58 us
    unnamed x27 -> x5, local copies, waits for them, and re-layouts: 6.65 us -> 3 us
    pallas_call x1, Pallas kernels: 59.8 us -> 58 us  [on_device(): pl.pallas_call(functools.partial(kernel, nz, nq, nx, coupling), out_shape...]
where the time goes in v4:
time: 62.6 us; the launch traced here: 62.3 us
  Pallas kernels  58 us (93%)
  local copies, waits for them, and re-layouts  3 us (5%)
  between operations  1.3 us (2%)
    pallas_call x1, Pallas kernels, on_device(): pl.pallas_call(functools.partial(kernel, nz, nq, nx, coupling), out_shape...  58 us
    unnamed x5, local copies, waits for them, and re-layouts  3 us

profile of v4, /device:TPU:1, one launch (start us, length us, event | category | flops | bytes accessed | tf_op | source)
XLA Modules:
  0.0 62.3 jit_solution(13950798976600882614)
XLA Ops:
  1.3 58.0 %shard_map.148 = (f32[1,128]{1,0:T(1,128)}, f32[3,128]{1,0:T(4,128)}, f32[3,512]{1,0:T(4,128)}) custom-call(f32[3,128]{1,0:T(4,128)} %qm_hbm.1, s32[1,128]{1,0:T(1,128)} %bitcast.15, s32[1,1]{1,0:T(1,128)} %bitcast.9.count_hbm, s32[4,128]{1,0:T(4,128)} %bitcast.10, s32[4,128]{1,0:T(4,128)} %bitcast.11, f32[3,512]{1,0:T(4,128)} %mm_hbm.1, f32[1,512]{1,0:T(1,128)} %bitcast.12, ...), custom_call_target="tpu_custom_call" | custom-call | tf_op jit(solution)/shard_map/pallas_call | solution.py:509
  59.3 0.0 copy-start
  59.3 1.2 %copy.20 = f32[128]{0:T(128)} copy(f32[128]{0:T(128)} %bitcast.17) | data formatting | bytes 1024
  60.5 1.2 %copy.21 = f32[3,128]{1,0:T(4,128)} copy(f32[3,128]{1,0:T(4,128)} %get-tuple-element.13) | data formatting | bytes 3072
  61.7 0.0 copy-done
  61.7 0.6 copy.22
Async XLA Ops:
  59.3 2.4 %copy-start = (f32[3,512]{1,0:T(4,128)S(1)}, f32[3,512]{1,0:T(4,128)}, u32[]{:S(2)}) copy-start(f32[3,512]{1,0:T(4,128)} %get-tuple-element.14) | copy-start | bytes 18436

commit v5 on v4

--- a/solution.py
+++ b/solution.py
@@ -10,13 +10,14 @@
 SOFTEN = 0.25
 LANES = 128
 FORCE_ROWS = 32
-EARLY = 2
+EARLY = 1
+LATE = 1
 TABLE = 7
 MESH = pl.DeviceIdType.MESH
 F32 = jnp.float32
 BF16 = jnp.bfloat16
 
-QM_N, MM_Q, POT_X, POT_Z, POT_Q, GRAD_Q, GRAD_N, QMF_Z, QMF_X, MMF_Q = range(10)
+QM_N, MM_Q, POT_X, POT_Z, POT_Q, GRAD_Q, GRAD_N, QMF_Z, QMF_X, MMF_Q, CODE_Q = range(11)
 
 
 def split3(value):
@@ -53,6 +54,7 @@
     pot_x,
     pot_z,
     pot_q,
+    code_q,
     grad_mine,
     grad_q,
     grad_n,
@@ -69,6 +71,8 @@
     acc_y,
     acc_z,
     inverses,
+    cube_high,
+    cube_low,
     mm_parts,
     charges,
     qm_lines,
@@ -111,13 +115,19 @@
     def shift(d):
         return (d + 1) // 2 * (2 * (d % 2) - 1)
 
+    def zigzag(k):
+        return k // 2 * (1 - 2 * (k % 2))
+
+    def reach(d):
+        return nz + zigzag(rings - d)
+
     def q_place(d, sign):
         y = (q // 2 + (nq // 2) + sign * (d // 2)) % (nq // 2)
         return y * 2 + (q + d) % 2
 
     same = lambda p: p
     near = (nz, ring, lambda d: (ring + rings - shift(d)) % rings, lambda d: (ring + rings + shift(d)) % rings, at_ring, lambda p: p % nz)
-    far = (rings, ring, lambda d: (ring + d) % rings, lambda d: (ring + rings - d) % rings, at_ring, same)
+    far = (rings, ring, lambda d: (ring + reach(d)) % rings, lambda d: (ring + rings - reach(d)) % rings, at_ring, same)
     plane = (nq, q, lambda d: q_place(d, 1), lambda d: q_place(d, -1), at_q, same)
     row_x = (nx, x, lambda d: (x + d) % nx, lambda d: (x + nx - d) % nx, lambda p: (blk, p * 2 + rep % 2), same)
 
@@ -144,7 +154,7 @@
         return copy_to(stage, d, device(p), src_of(p), buffer.at[slot(mine)])
 
     def send_all(stage, axis, src_of, buffer):
-        each(axis, lambda d: outgoing(stage, axis, src_of, buffer, d).start())
+        each(axis, lambda d: outgoing(stage, axis, src_of, buffer, axis[0] - d).start())
 
     def sent_all(stage, axis, src_of, buffer):
         each(axis, lambda d: outgoing(stage, axis, src_of, buffer, d).wait_send())
@@ -187,9 +197,6 @@
             ]
         )
     ]
-    for fetch in fetches:
-        fetch.start()
-
     barrier = pltpu.get_barrier_semaphore()
     def greet(device):
         pl.semaphore_signal(barrier, inc=1, device_id=device, device_id_type=MESH)
@@ -202,6 +209,8 @@
     lax.fori_loop(1, nz // 2 + 1, greet_ring, 0)
     each(plane, lambda d: greet(at_q(plane[2](d))))
     each(row_x, lambda d: greet(row_x[4](row_x[2](d))))
+    for fetch in fetches:
+        fetch.start()
     for fetch in fetches[:5]:
         fetch.wait()
 
@@ -245,7 +254,6 @@
         wide_x[rows, :] = wide(qm_all[p, 0:1, :])
         wide_y[rows, :] = wide(qm_all[p, 1:2, :])
         wide_z[rows, :] = wide(qm_all[p, 2:3, :])
-        pot_q[q, pl.ds(nz + p, 1), :] = qm_all[p, 3:4, :]
         return carry
 
     def chunk_columns(p):
@@ -306,6 +314,9 @@
         return jnp.sum(jnp.transpose(acc[block_rows(p), :]), axis=0, keepdims=True)
 
     send_all(POT_X, row_x, lambda p: pot_x.at[x], pot_x)
+    for p in range(nz):
+        code_q[q, p : p + 1, :] = qm_all[p, 3:4, :]
+    send_all(CODE_Q, plane, lambda p: code_q.at[q], code_q)
     acc_x[...] = jnp.zeros_like(acc_x)
     acc_y[...] = jnp.zeros_like(acc_y)
     acc_z[...] = jnp.zeros_like(acc_z)
@@ -341,11 +352,14 @@
     wait_all(POT_X, row_x, pot_x)
     pot_z[ring] = total(pot_x, nx)
     send_all(POT_Z, far, lambda p: pot_z.at[ring], pot_z)
-    lax.fori_loop(early, nq, pull_chunk, 0)
+    late = max(early, nq - LATE)
+    lax.fori_loop(early, late, pull_chunk, 0)
 
     wait_all(POT_Z, far, pot_z)
-    pot_q[q, 0:nz, :] = total(pot_z, rings) * coupling
+    pot_q[q] = total(pot_z, rings) * coupling
     send_all(POT_Q, plane, lambda p: pot_q.at[q], pot_q)
+    lax.fori_loop(late, nq, pull_chunk, 0)
+
     def gather_force(p, carry):
         qmf_mine[p, 0:1, :] = lines(acc_x, p)
         qmf_mine[p, 1:2, :] = lines(acc_y, p)
@@ -355,13 +369,21 @@
     lax.fori_loop(0, nz, gather_force, 0)
     qmf_z[ring] = qmf_mine[z]
     send_all(QMF_Z, far, lambda p: qmf_mine.at[p % nz], qmf_z)
-    wait_all(POT_Q, plane, pot_q)
-
-    potentials = jnp.concatenate([pot_q[p, 0:nz, :] for p in range(nq)], axis=0)
-    codes = jnp.concatenate([pot_q[p, nz : 2 * nz, :] for p in range(nq)], axis=0)
+
+    wait_all(CODE_Q, plane, code_q)
+    codes = jnp.concatenate([code_q[p] for p in range(nq)], axis=0).astype(BF16)
     gain = gain_ref[...]
     table = table_wide[...].astype(BF16)
-    pieces = [*split3(potentials), codes.astype(BF16)]
+    bases, lives = [], []
+    for k in range(neighbours + 1):
+        rows = slice(k * atoms, (k + 1) * atoms)
+        picked = jnp.dot(owner_hot[rows, 0:blocks], codes, preferred_element_type=F32)
+        code = jnp.sum(picked * slot_hot[rows, :], axis=1, keepdims=True)
+        lives.append((code >= 0).astype(F32))
+        kinds = (lane.astype(F32) == code).astype(F32).astype(BF16)
+        bases.append(jnp.dot(kinds, table, preferred_element_type=F32))
+    wait_all(POT_Q, plane, pot_q)
+    pieces = split3(jnp.concatenate([pot_q[p] for p in range(nq)], axis=0))
     neighbour = jnp.zeros((atoms, LANES), F32)
     for k in range(neighbours + 1):
         rows = slice(k * atoms, (k + 1) * atoms)
@@ -369,11 +391,8 @@
         slots = slot_hot[rows, :]
         picked = [jnp.dot(hot, piece, preferred_element_type=F32) for piece in pieces]
         potential = jnp.sum((picked[0] + picked[1] + picked[2]) * slots, axis=1, keepdims=True)
-        code = jnp.sum(picked[3] * slots, axis=1, keepdims=True)
-        live = (code >= 0).astype(F32)
-        kinds = (lane.astype(F32) == code).astype(F32).astype(BF16)
-        base = jnp.dot(kinds, table, preferred_element_type=F32)
-        start = (live * (base + potential * gain)).astype(BF16)
+        live = lives[k]
+        start = (live * (bases[k] + potential * gain)).astype(BF16)
         if k < neighbours:
             neighbour = neighbour + start.astype(F32)
     mixed = start.astype(F32) + jnp.dot(
@@ -412,6 +431,16 @@
     atom_energy_ref[...] = jnp.sum(
         jnp.where(lane == row, atom_energy, 0.0), axis=0, keepdims=True
     )
+
+    def split_rows(g, carry):
+        rows = pl.ds(pl.multiple_of(g * FORCE_ROWS, FORCE_ROWS), FORCE_ROWS)
+        cube = inverses[rows, :]
+        high = cube.astype(BF16)
+        cube_high[rows, :] = high
+        cube_low[rows, :] = (cube - high.astype(F32)).astype(BF16)
+        return carry
+
+    lax.fori_loop(0, nz * atoms // FORCE_ROWS, split_rows, 0)
     wait_all(GRAD_Q, plane, grad_q)
     grad_n[z] = total(grad_q, nq)
     send_all(GRAD_N, near, lambda p: grad_n.at[z], grad_n)
@@ -419,7 +448,7 @@
     qmf_x[x] = total(qmf_z, rings)
     send_all(QMF_X, row_x, lambda p: qmf_x.at[x], qmf_x)
     wait_all(GRAD_N, near, grad_n)
-    live_plane = (pot_q[q, nz : 2 * nz, :] >= 0).astype(F32)
+    live_plane = (code_q[q] >= 0).astype(F32)
     grad_sum[...] = live_plane * total(grad_n, nz)
 
     effective = jnp.concatenate([grad_sum[p : p + 1, :] for p in range(nz)], axis=1)
@@ -427,31 +456,35 @@
     high = weights.astype(BF16).astype(F32)
     weights = jnp.concatenate([high, weights - high], axis=0).astype(BF16)
 
-    def push_chunk(step, carry):
-        d = nq - step
-        chunk = jnp.where(d > 0, plane[2](d), q)
-
-        cube = inverses[:, chunk_columns(chunk)]
-        high = cube.astype(BF16)
-        low = (cube - high.astype(F32)).astype(BF16)
-        sums = jnp.dot(weights, high, preferred_element_type=F32)
-        sums = sums + jnp.dot(weights, low, preferred_element_type=F32)
+    def push_pair(y):
+        width = 2 * mm_tiles * LANES
+        where = pl.ds(pl.multiple_of(y * width, width), width)
+        sums = jnp.dot(weights, cube_high[:, where], preferred_element_type=F32)
+        sums = sums + jnp.dot(weights, cube_low[:, where], preferred_element_type=F32)
         sums = sums[0:8, :] + sums[8:16, :]
-        mmf_mine[chunk] = sums[1:4, :] - sums[0:1, :] * mm_all[chunk, 0:3, :]
-
-        @pl.when(d > 0)
-        def _():
-            outgoing(MMF_Q, plane, lambda p: mmf_mine.at[p], mmf_q, d).start()
-
+        for c in range(2):
+            part = sums[:, c * width // 2 : (c + 1) * width // 2]
+            mmf_mine[2 * y + c] = part[1:4, :] - part[0:1, :] * mm_all[2 * y + c, 0:3, :]
+
+    rows_y = nq // 2
+
+    def push_step(k, carry):
+        step = rows_y // 2 + zigzag(k)
+        push_pair((q // 2 + step) % rows_y)
+        for c in range(2):
+            outgoing(MMF_Q, plane, lambda p: mmf_mine.at[p], mmf_q, 2 * step + c).start()
         return carry
 
-    lax.fori_loop(1, nq + 1, push_chunk, 0)
+    lax.fori_loop(1, rows_y, push_step, 0)
+    push_pair(q // 2)
+    outgoing(MMF_Q, plane, lambda p: mmf_mine.at[p], mmf_q, 1).start()
     mmf_q[q] = mmf_mine[q]
     sent_all(QM_N, near, lambda p: qm_all.at[z], qm_all)
     sent_all(MM_Q, plane, lambda p: mm_all.at[q], mm_all)
     sent_all(POT_X, row_x, lambda p: pot_x.at[x], pot_x)
     sent_all(POT_Z, far, lambda p: pot_z.at[ring], pot_z)
     sent_all(POT_Q, plane, lambda p: pot_q.at[q], pot_q)
+    sent_all(CODE_Q, plane, lambda p: code_q.at[q], code_q)
     sent_all(QMF_Z, far, lambda p: qmf_mine.at[p % nz], qmf_z)
     sent_all(GRAD_Q, plane, lambda p: grad_mine.at[p], grad_q)
     sent_all(GRAD_N, near, lambda p: grad_n.at[z], grad_n)
@@ -520,7 +553,8 @@
             small(nz, 4, atoms),
             small(nx, nz, atoms),
             small(2 * nz, nz, atoms),
-            small(nq, 2 * nz, atoms),
+            small(nq, nz, atoms),
+            small(nq, nz, atoms),
             small(nq, nz, atoms),
             small(nq, nz, atoms),
             small(nz, nz, atoms),
@@ -532,6 +566,8 @@
             small(nq, 3, mm_here),
             *[small(here, LANES)] * 6,
             small(here, nq * mm_here),
+            pltpu.VMEM((here, nq * mm_here), BF16),
+            pltpu.VMEM((here, nq * mm_here), BF16),
             pltpu.VMEM((48, nq * mm_here), BF16),
             small(1, nq * mm_here),
             small(8, here),
@@ -541,8 +577,8 @@
             small(groups * atoms, LANES),
             *[pltpu.VMEM(a.shape, a.dtype) for k, a in enumerate(arguments) if k != TABLE],
             pltpu.SemaphoreType.DMA((12,)),
-            pltpu.SemaphoreType.DMA((10, max(2 * nz, nq, nx))),
-            pltpu.SemaphoreType.DMA((10, max(2 * nz, nq, nx))),
+            pltpu.SemaphoreType.DMA((11, max(2 * nz, nq, nx))),
+            pltpu.SemaphoreType.DMA((11, max(2 * nz, nq, nx))),
         ],
         compiler_params=pltpu.CompilerParams(
             collective_id=0, has_side_effects=True, vmem_limit_bytes=56 * 2**20

time: 62.6 us -> 61.9 us (0.989)
  no operation moved by 1% of the time
where the time goes in v5:
time: 61.9 us; the launch traced here: 61.7 us
  Pallas kernels  57.4 us (93%)
  local copies, waits for them, and re-layouts  3 us (5%)
  between operations  1.3 us (2%)
    pallas_call x1, Pallas kernels, on_device(): pl.pallas_call(functools.partial(kernel, nz, nq, nx, coupling), out_shape...  57.4 us
    unnamed x5, local copies, waits for them, and re-layouts  3 us

profile of v5, /device:TPU:1, one launch (start us, length us, event | category | flops | bytes accessed | tf_op | source)
XLA Modules:
  0.0 61.7 jit_solution(16212034504939831491)
XLA Ops:
  1.3 57.4 %shard_map.148 = (f32[1,128]{1,0:T(1,128)}, f32[3,128]{1,0:T(4,128)}, f32[3,512]{1,0:T(4,128)}) custom-call(f32[3,128]{1,0:T(4,128)} %qm_hbm.1, s32[1,128]{1,0:T(1,128)} %bitcast.15, s32[1,1]{1,0:T(1,128)} %bitcast.9.count_hbm, s32[4,128]{1,0:T(4,128)} %bitcast.10, s32[4,128]{1,0:T(4,128)} %bitcast.11, f32[3,512]{1,0:T(4,128)} %mm_hbm.1, f32[1,512]{1,0:T(1,128)} %bitcast.12, ...), custom_call_target="tpu_custom_call" | custom-call | tf_op jit(solution)/shard_map/pallas_call | solution.py:542
  58.7 0.0 copy-start
  58.7 1.2 %copy.20 = f32[128]{0:T(128)} copy(f32[128]{0:T(128)} %bitcast.17) | data formatting | bytes 1024
  59.8 1.2 %copy.21 = f32[3,128]{1,0:T(4,128)} copy(f32[3,128]{1,0:T(4,128)} %get-tuple-element.13) | data formatting | bytes 3072
  61.1 0.0 copy-done
  61.1 0.6 copy.22
Async XLA Ops:
  58.7 2.4 %copy-start = (f32[3,512]{1,0:T(4,128)S(1)}, f32[3,512]{1,0:T(4,128)}, u32[]{:S(2)}) copy-start(f32[3,512]{1,0:T(4,128)} %get-tuple-element.14) | copy-start | bytes 18436

commit v6 on v5

--- a/solution.py
+++ b/solution.py
@@ -581,7 +581,7 @@
             pltpu.SemaphoreType.DMA((11, max(2 * nz, nq, nx))),
         ],
         compiler_params=pltpu.CompilerParams(
-            collective_id=0, has_side_effects=True, vmem_limit_bytes=56 * 2**20
+            collective_id=0, has_side_effects=True, vmem_limit_bytes=55176 * 2**10
         ),
     )(*arguments)
     return (atom_energy[0], qm_force, mm_force)

time: 61.9 us -> 60.3 us (0.974)
  Pallas kernels: 57.4 us -> 56.3 us
    pallas_call x1, Pallas kernels: 57.4 us -> 56.3 us  [on_device(): pl.pallas_call(functools.partial(kernel, nz, nq, nx, coupling), out_shape...]
    unnamed x5 -> x21, local copies, waits for them, and re-layouts: 3 us -> 2.42 us
where the time goes in v6:
time: 60.3 us; the launch traced here: 60.1 us
  Pallas kernels  56.3 us (93%)
  local copies, waits for them, and re-layouts  2.42 us (4%)
  between operations  1.37 us (2%)
    pallas_call x1, Pallas kernels, on_device(): pl.pallas_call(functools.partial(kernel, nz, nq, nx, coupling), out_shape...  56.3 us
    unnamed x21, local copies, waits for them, and re-layouts  2.42 us

profile of v6, /device:TPU:1, one launch (start us, length us, event | category | flops | bytes accessed | tf_op | source)
XLA Modules:
  0.0 60.1 jit_solution(2099070655521907154)
XLA Ops:
  1.3 0.0 copy-start.6
  1.3 0.0 copy-start.7
  1.3 0.0 copy-start.8
  1.3 0.0 copy-start.4
  1.3 0.0 copy-start.3
  1.3 0.0 copy-start.2
  1.3 0.0 copy-start.1
  1.4 0.0 copy-start
  1.4 0.0 copy-start.5
  1.4 0.6 copy-done.6
  2.0 0.0 copy-done.7
  2.0 0.0 copy-done.8
  2.0 0.0 copy-done.4
  2.0 0.0 copy-done.3
  2.0 0.0 copy-done.2
  2.0 0.0 copy-done.1
  2.1 0.0 copy-done
  2.1 0.0 copy-done.5
  2.1 56.3 %shard_map.148 = (f32[1,128]{1,0:T(1,128)S(1)}, f32[3,128]{1,0:T(4,128)S(1)}, f32[3,512]{1,0:T(4,128)S(1)}) custom-call(f32[3,128]{1,0:T(4,128)S(1)} %copy-done, s32[1,128]{1,0:T(1,128)S(1)} %bitcast.15, s32[1,1]{1,0:T(1,128)} %bitcast.9.count_hbm, s32[4,128]{1,0:T(4,128)S(1)} %bitcast.10, s32[4,128]{1,0:T(4,128)S(1)} %bitcast.11, f32[3,512]{1,0:T(4,128)} %mm_hbm.1, ...), custom_call_target="tpu_custom_call" | custom-call | tf_op jit(solution)/shard_map/pallas_call | solution.py:542
  58.4 0.5 copy.20
  58.9 0.6 copy.21
  59.5 0.6 copy.22
Async XLA Ops:
  1.3 0.7 %copy-start.6 = (f32[256]{0:T(256)S(1)}, f32[256]{0:T(256)}, u32[]{:S(2)}) copy-start(f32[256]{0:T(256)} %param.25) | copy-start | bytes 3076
  1.3 0.7 %copy-start.7 = (s32[128]{0:T(128)S(1)}, s32[128]{0:T(128)}, u32[]{:S(2)}) copy-start(s32[128]{0:T(128)} %param.14) | copy-start | bytes 1540
  1.3 0.7 %copy-start.8 = (f32[128]{0:T(128)S(1)}, f32[128]{0:T(128)}, u32[]{:S(2)}) copy-start(f32[128]{0:T(128)} %param.21) | copy-start | bytes 1540
  1.3 0.7 %copy-start.4 = (bf16[8,128]{1,0:T(8,128)(2,1)S(1)}, bf16[8,128]{1,0:T(8,128)(2,1)}, u32[]{:S(2)}) copy-start(bf16[8,128]{1,0:T(8,128)(2,1)} %table_ref.1) | copy-start | bytes 6148
  1.3 0.7 %copy-start.3 = (f32[512]{0:T(512)S(1)}, f32[512]{0:T(512)}, u32[]{:S(2)}) copy-start(f32[512]{0:T(512)} %param.19) | copy-start | bytes 6148
  1.3 0.7 %copy-start.2 = (s32[128,4]{0,1:T(4,128)S(1)}, s32[128,4]{0,1:T(4,128)}, u32[]{:S(2)}) copy-start(s32[128,4]{0,1:T(4,128)} %param.17) | copy-start | bytes 6148
  1.3 0.7 %copy-start.1 = (s32[128,4]{0,1:T(4,128)S(1)}, s32[128,4]{0,1:T(4,128)}, u32[]{:S(2)}) copy-start(s32[128,4]{0,1:T(4,128)} %param.16) | copy-start | bytes 6148
  1.4 0.7 %copy-start = (f32[3,128]{1,0:T(4,128)S(1)}, f32[3,128]{1,0:T(4,128)}, u32[]{:S(2)}) copy-start(f32[3,128]{1,0:T(4,128)} %qm_hbm.1) | copy-start | bytes 4612
  1.4 0.7 %copy-start.5 = (f32[256]{0:T(256)S(1)}, f32[256]{0:T(256)}, u32[]{:S(2)}) copy-start(f32[256]{0:T(256)} %param.24) | copy-start | bytes 3076

commit v7 on v6

--- a/solution.py
+++ b/solution.py
@@ -302,7 +302,8 @@
             pot_x[x, pl.ds(p, 1), :] = jnp.sum(jnp.transpose(running[rows, :]), axis=0, keepdims=True)
         return carry
 
-    lax.fori_loop(0, nz // 2, potential_step, 0)
+    for k in range(nz // 2):
+        potential_step(k, 0)
 
     def columns(chunk):
         return [

time: 60.3 us -> 60.2 us (level)
  no operation moved by 1% of the time
where the time goes in v7:
time: 60.2 us; the launch traced here: 60 us
  Pallas kernels  56.2 us (93%)
  local copies, waits for them, and re-layouts  2.42 us (4%)
  between operations  1.37 us (2%)
    pallas_call x1, Pallas kernels, on_device(): pl.pallas_call(functools.partial(kernel, nz, nq, nx, coupling), out_shape...  56.2 us
    unnamed x21, local copies, waits for them, and re-layouts  2.42 us

profile of v7, /device:TPU:1, one launch (start us, length us, event | category | flops | bytes accessed | tf_op | source)
XLA Modules:
  0.0 60.0 jit_solution(9494100606884532952)
XLA Ops:
  1.3 0.0 copy-start.6
  1.3 0.0 copy-start.7
  1.3 0.0 copy-start.8
  1.3 0.0 copy-start.4
  1.3 0.0 copy-start.3
  1.3 0.0 copy-start.2
  1.3 0.0 copy-start.1
  1.4 0.0 copy-start
  1.4 0.0 copy-start.5
  1.4 0.6 copy-done.6
  2.0 0.0 copy-done.7
  2.0 0.0 copy-done.8
  2.0 0.0 copy-done.4
  2.0 0.0 copy-done.3
  2.0 0.0 copy-done.2
  2.0 0.0 copy-done.1
  2.1 0.0 copy-done
  2.1 0.0 copy-done.5
  2.1 56.2 %shard_map.148 = (f32[1,128]{1,0:T(1,128)S(1)}, f32[3,128]{1,0:T(4,128)S(1)}, f32[3,512]{1,0:T(4,128)S(1)}) custom-call(f32[3,128]{1,0:T(4,128)S(1)} %copy-done, s32[1,128]{1,0:T(1,128)S(1)} %bitcast.15, s32[1,1]{1,0:T(1,128)} %bitcast.9.count_hbm, s32[4,128]{1,0:T(4,128)S(1)} %bitcast.10, s32[4,128]{1,0:T(4,128)S(1)} %bitcast.11, f32[3,512]{1,0:T(4,128)} %mm_hbm.1, ...), custom_call_target="tpu_custom_call" | custom-call | tf_op jit(solution)/shard_map/pallas_call | solution.py:543
  58.3 0.5 copy.20
  58.8 0.6 copy.21
  59.4 0.6 copy.22
Async XLA Ops:
  1.3 0.7 %copy-start.6 = (f32[256]{0:T(256)S(1)}, f32[256]{0:T(256)}, u32[]{:S(2)}) copy-start(f32[256]{0:T(256)} %param.25) | copy-start | bytes 3076
  1.3 0.7 %copy-start.7 = (s32[128]{0:T(128)S(1)}, s32[128]{0:T(128)}, u32[]{:S(2)}) copy-start(s32[128]{0:T(128)} %param.14) | copy-start | bytes 1540
  1.3 0.7 %copy-start.8 = (f32[128]{0:T(128)S(1)}, f32[128]{0:T(128)}, u32[]{:S(2)}) copy-start(f32[128]{0:T(128)} %param.21) | copy-start | bytes 1540
  1.3 0.7 %copy-start.4 = (bf16[8,128]{1,0:T(8,128)(2,1)S(1)}, bf16[8,128]{1,0:T(8,128)(2,1)}, u32[]{:S(2)}) copy-start(bf16[8,128]{1,0:T(8,128)(2,1)} %table_ref.1) | copy-start | bytes 6148
  1.3 0.7 %copy-start.3 = (f32[512]{0:T(512)S(1)}, f32[512]{0:T(512)}, u32[]{:S(2)}) copy-start(f32[512]{0:T(512)} %param.19) | copy-start | bytes 6148
  1.3 0.7 %copy-start.2 = (s32[128,4]{0,1:T(4,128)S(1)}, s32[128,4]{0,1:T(4,128)}, u32[]{:S(2)}) copy-start(s32[128,4]{0,1:T(4,128)} %param.17) | copy-start | bytes 6148
  1.3 0.7 %copy-start.1 = (s32[128,4]{0,1:T(4,128)S(1)}, s32[128,4]{0,1:T(4,128)}, u32[]{:S(2)}) copy-start(s32[128,4]{0,1:T(4,128)} %param.16) | copy-start | bytes 6148
  1.4 0.7 %copy-start = (f32[3,128]{1,0:T(4,128)S(1)}, f32[3,128]{1,0:T(4,128)}, u32[]{:S(2)}) copy-start(f32[3,128]{1,0:T(4,128)} %qm_hbm.1) | copy-start | bytes 4612
  1.4 0.7 %copy-start.5 = (f32[256]{0:T(256)S(1)}, f32[256]{0:T(256)}, u32[]{:S(2)}) copy-start(f32[256]{0:T(256)} %param.24) | copy-start | bytes 3076
